TPU v7x, 256 devices: a whole 4x4x8 slice. The times are simulated.
256 devices in a mesh: ctx: 16 (over z_hi, y, core), chan: 16 (over z_lo, x).
Axes of the slice: x: 4, y: 4, z: 8 (z_hi: 2, z_lo: 4; z = z_hi * 4 + z_lo), core: 2. Of those that a mesh axis runs over, the one named last changes fastest.
Arguments:
- signal: bfloat16 [4096, 2048], P('chan', 'ctx'), may hold values from -6 to 6
- gating: bfloat16 [4096, 2048], P('chan', 'ctx'), may hold values from -6 to 6
- skip_gain: float32 [4096], P('chan'), may hold values from -4 to 4
- spectrum: float32 [2, 4096, 32, 128], P(None, 'chan', 'ctx'), may hold values from -6 to 6
- out_weight: bfloat16 [4096, 4096], P(None, 'chan'), may hold values from -0.125 to 0.125
- cotangent: bfloat16 [2048, 4096], P('ctx', 'chan'), may hold values from -1.5 to 1.5
Outputs:
- output: bfloat16 [2048, 4096], P('ctx', 'chan')
- grad_signal: bfloat16 [4096, 2048], P('chan', 'ctx')
- grad_gating: bfloat16 [4096, 2048], P('chan', 'ctx')
- grad_spectrum: float32 [2, 4096, 32, 128], P(None, 'chan', 'ctx')
All inputs are finite; a program needn't handle non-finite values.
Results may differ from a plain program's by a relative error of at most 0.0054.
Values may be sent and summed in bfloat16 or wider, within the bound.
No kernel may reach another device: no remote copies, remote signals or barrier semaphores. Data moves between devices by JAX's collectives and lax.ppermute only.
A program may use at most 64 MiB of HBM per device.

v0:
```python
import math

import jax
import jax.numpy as jnp
import numpy as np
from jax import lax
from jax.experimental import pallas as pl
from jax.experimental.pallas import tpu as pltpu
from jax.sharding import PartitionSpec as P

F32 = jnp.float32
BF16 = jnp.bfloat16
HIGHEST = lax.Precision.HIGHEST
VMEM = pl.BlockSpec(memory_space=pltpu.VMEM)
SMEM = pl.BlockSpec(memory_space=pltpu.SMEM)

N_CTX = 16
N_CHAN = 16
SPAN = 128
FULL = 2 * N_CTX * SPAN


def swap(block, axis, mask):
    return lax.ppermute(block, axis, [(i, i ^ mask) for i in range(16)])


def rev4(number):
    return int(f"{number:04b}"[::-1], 2)


def phase(turns, modulus):
    angle = (turns % modulus) * (2.0 * math.pi / modulus)
    return np.cos(angle), np.sin(angle)


def tables():
    ranks = np.arange(N_CTX)
    residues = np.array([[2 * rev4(r) + e for e in range(2)] for r in ranks])
    slots = ranks[:, None] ^ ranks[None, :]
    turn = np.stack(phase(slots[:, None, :] * residues[:, :, None], 32), 1)
    twid = np.stack(phase(residues[:, :, None] * np.arange(SPAN), FULL), 1)
    cos, sin = phase(np.arange(SPAN)[:, None] * np.arange(SPAN), SPAN)
    inner = np.block([[cos, -sin], [sin, cos]])
    return (
        turn.reshape(N_CTX, 64).astype(np.float32),
        twid.reshape(N_CTX, 4, SPAN).astype(np.float32),
        inner.astype(np.float32),
    )


def cost(flops, moved):
    return pl.CostEstimate(flops=flops, bytes_accessed=moved, transcendentals=0)


CHUNK = 32


def spread(slot_refs, turn_ref, twid_ref, held_ref):
    rows = held_ref.shape[1]

    def step(n, _):
        at = pl.ds(pl.multiple_of(n * CHUNK, CHUNK), CHUNK)
        acc = [jnp.zeros((CHUNK, SPAN), F32) for _ in range(4)]
        for i, (ref, place) in enumerate(slot_refs):
            x = (ref[at, :] if place is None else ref[place, at, :]).astype(F32)
            for e in range(2):
                acc[2 * e] += x * turn_ref[e * 16 + i]
                acc[2 * e + 1] -= x * turn_ref[32 + e * 16 + i]
        for e in range(2):
            re, im = acc[2 * e], acc[2 * e + 1]
            cos, sin = twid_ref[pl.ds(e, 1), :], twid_ref[pl.ds(2 + e, 1), :]
            held_ref[e, at, pl.ds(0, SPAN)] = re * cos + im * sin
            held_ref[e, at, pl.ds(SPAN, SPAN)] = im * cos - re * sin
        return _

    lax.fori_loop(0, rows // CHUNK, step, None)


def merge(held_ref, turn_ref, twid_ref, keep_ref, send_ref):
    rows = held_ref.shape[1]

    def step(n, _):
        at = pl.ds(pl.multiple_of(n * CHUNK, CHUNK), CHUNK)
        turned = []
        for e in range(2):
            re = held_ref[e, at, pl.ds(0, SPAN)] * (1.0 / FULL)
            im = held_ref[e, at, pl.ds(SPAN, SPAN)] * (1.0 / FULL)
            cos, sin = twid_ref[pl.ds(e, 1), :], twid_ref[pl.ds(2 + e, 1), :]
            turned.append((re * cos - im * sin, re * sin + im * cos))
        for i in range(16):
            total = jnp.zeros((CHUNK, SPAN), F32)
            for e in range(2):
                total += turned[e][0] * turn_ref[e * 16 + i]
                total -= turned[e][1] * turn_ref[32 + e * 16 + i]
            out = send_ref if i % 2 else keep_ref
            out[i // 2, at, :] = total.astype(out.dtype)
        return _

    lax.fori_loop(0, rows // CHUNK, step, None)


def dft(held, inner):
    return jnp.dot(held, inner, precision=HIGHEST, preferred_element_type=F32)


def idft(held, inner):
    return lax.dot_general(
        held, inner, (((1,), (1,)), ((), ())), precision=HIGHEST, preferred_element_type=F32
    )


def slot_list(refs):
    slots = {}
    for core in range(2):
        own, far, *pairs = refs[5 * core : 5 * core + 5]
        slots[core] = (own, None)
        slots[8 + core] = (far, None)
        for ky, pair in enumerate(pairs, 1):
            slots[2 * ky + core] = (pair, 0)
            slots[8 + 2 * ky + core] = (pair, 1)
    return [slots[i] for i in range(16)]


def forward_kernel(turn_ref, twid_ref, inner_ref, filt_ref, *refs):
    slot_refs = slot_list(refs[:10])
    freq_ref, keep_ref, send_ref, held_ref = refs[10:]
    spread(slot_refs, turn_ref, twid_ref, held_ref)
    for e in range(2):
        freq = dft(held_ref[e], inner_ref[...])
        freq_ref[e] = freq
        re, im = freq[:, :SPAN], freq[:, SPAN:]
        filt_re, filt_im = filt_ref[0, e], filt_ref[1, e]
        prod = jnp.concatenate([filt_re * re - filt_im * im, filt_re * im + filt_im * re], 1)
        held_ref[e] = idft(prod, inner_ref[...])
    merge(held_ref, turn_ref, twid_ref, keep_ref, send_ref)


def backward_kernel(turn_ref, twid_ref, inner_ref, filt_ref, sig_ref, *refs):
    slot_refs = slot_list(refs[:10])
    cross_ref, keep_ref, send_ref, held_ref = refs[10:]
    spread(slot_refs, turn_ref, twid_ref, held_ref)
    for e in range(2):
        freq = dft(held_ref[e], inner_ref[...])
        re, im = freq[:, :SPAN], freq[:, SPAN:]
        sig_re, sig_im = sig_ref[e, :, :SPAN], sig_ref[e, :, SPAN:]
        cross_ref[0, e] = (re * sig_re + im * sig_im) * (1.0 / FULL)
        cross_ref[1, e] = (im * sig_re - re * sig_im) * (1.0 / FULL)
        filt_re, filt_im = filt_ref[0, e], filt_ref[1, e]
        prod = jnp.concatenate([filt_re * re + filt_im * im, filt_re * im - filt_im * re], 1)
        held_ref[e] = idft(prod, inner_ref[...])
    merge(held_ref, turn_ref, twid_ref, keep_ref, send_ref)


PARAMS = pltpu.CompilerParams(vmem_limit_bytes=32 * 1024 * 1024)


def forward_call(consts, filt, blocks, send_type):
    rows = filt.shape[2]
    return pl.pallas_call(
        forward_kernel,
        out_shape=(
            jax.ShapeDtypeStruct((2, rows, 2 * SPAN), F32),
            jax.ShapeDtypeStruct((8, rows, SPAN), F32),
            jax.ShapeDtypeStruct((8, rows, SPAN), send_type),
        ),
        in_specs=[SMEM] + [VMEM] * 13,
        out_specs=(VMEM,) * 3,
        scratch_shapes=[pltpu.VMEM((2, rows, 2 * SPAN), F32)],
        compiler_params=PARAMS,
        cost_estimate=cost(2_000_000_000, 4 << 20),
        name="forward_transform",
    )(*consts, filt, *blocks)


def backward_call(consts, filt, sig_freq, blocks, send_type):
    rows = filt.shape[2]
    return pl.pallas_call(
        backward_kernel,
        out_shape=(
            jax.ShapeDtypeStruct((2, 2, rows, SPAN), F32),
            jax.ShapeDtypeStruct((8, rows, SPAN), F32),
            jax.ShapeDtypeStruct((8, rows, SPAN), send_type),
        ),
        in_specs=[SMEM] + [VMEM] * 14,
        out_specs=(VMEM,) * 3,
        scratch_shapes=[pltpu.VMEM((2, rows, 2 * SPAN), F32)],
        compiler_params=PARAMS,
        cost_estimate=cost(2_000_000_000, 4 << 20),
        name="backward_transform",
    )(*consts, filt, sig_freq, *blocks)


def weight_rows(weight_ref, place_ref, kx, kz, rows):
    start = (place_ref[0] ^ kz) * 4 + (place_ref[1] ^ kx)
    return weight_ref[pl.ds(pl.multiple_of(start * rows, rows), rows), :]


def partial_kernel(place_ref, weight_ref, cot_ref, *out_refs):
    rows = out_refs[0].shape[1]
    for kx in (2, 1, 3, 0):
        for kz in range(4):
            out_refs[kx][kz] = lax.dot_general(
                weight_rows(weight_ref, place_ref, kx, kz, rows),
                cot_ref[...],
                (((1,), (1,)), ((), ())),
                preferred_element_type=F32,
            ).astype(BF16)


def partial_call(place, weight, cot):
    rows = weight.shape[0] // N_CHAN
    return pl.pallas_call(
        partial_kernel,
        out_shape=(jax.ShapeDtypeStruct((4, rows, cot.shape[0]), BF16),) * 4,
        in_specs=[SMEM, VMEM, VMEM],
        out_specs=(VMEM,) * 4,
        compiler_params=PARAMS,
        cost_estimate=cost(268_000_000, 3 << 20),
        name="partial_grad_mixed",
    )(place, weight, cot)


def project_kernel(place_ref, weight_ref, *refs):
    out_ref = refs[-1]
    total = None
    for kx in range(4):
        for kz in range(4):
            block = refs[kx][kz]
            term = lax.dot_general(
                block,
                weight_rows(weight_ref, place_ref, kx, kz, block.shape[0]),
                (((0,), (0,)), ((), ())),
                preferred_element_type=F32,
            )
            total = term if total is None else total + term
    out_ref[...] = total.astype(BF16)


def project_call(place, weight, groups):
    return pl.pallas_call(
        project_kernel,
        out_shape=jax.ShapeDtypeStruct((SPAN, weight.shape[1]), BF16),
        in_specs=[SMEM] + [VMEM] * 5,
        out_specs=VMEM,
        compiler_params=PARAMS,
        cost_estimate=cost(268_000_000, 3 << 20),
        name="project_output",
    )(place, weight, *groups)


def gather_ctx(block):
    far = swap(block, "ctx", 8)
    both = jnp.stack([block, far])
    held = [block, far] + [swap(both, "ctx", 2 * ky) for ky in (1, 2, 3)]
    return held + [swap(part, "ctx", 1) for part in held]


def reduce_ctx(keep, send):
    keep = keep + swap(send, "ctx", 1).astype(F32)
    keep = keep.reshape(2, 4, *keep.shape[1:])
    pairs = [swap(keep[:, ky].astype(BF16), "ctx", 2 * ky) for ky in (1, 2, 3)]
    total = keep[:, 0]
    for pair in pairs:
        total = total + pair.astype(F32)
    return total[0] + swap(total[1].astype(BF16), "ctx", 8).astype(F32)


def reduce_chan(parts):
    total = parts[0].astype(F32)
    for kx in (1, 2, 3):
        total = total + swap(parts[kx], "chan", kx).astype(F32)
    result = total[0]
    for kz in (1, 2, 3):
        result = result + swap(total[kz].astype(BF16), "chan", 4 * kz).astype(F32)
    return result


def gather_chan(block):
    group = jnp.stack([block] + [swap(block, "chan", 4 * kz) for kz in (1, 2, 3)])
    return [group] + [swap(group, "chan", kx) for kx in (1, 2, 3)]


def body(signal, gating, skip_gain, spectrum, out_weight, cotangent):
    ctx = lax.axis_index("ctx")
    chan = lax.axis_index("chan")
    place = jnp.stack([chan // 4, chan % 4]).astype(jnp.int32)
    turn, twid, inner = tables()
    consts = (
        lax.dynamic_index_in_dim(turn, ctx, 0, keepdims=False),
        lax.dynamic_index_in_dim(twid, ctx, 0, keepdims=False),
        jnp.asarray(inner),
    )
    gate = gating.astype(F32)
    skip = skip_gain[:, None]
    filt = jnp.transpose(spectrum, (0, 2, 1, 3))

    parts = partial_call(place, out_weight, cotangent)
    sig_blocks = gather_ctx(signal)
    grad_mixed = reduce_chan(parts)
    grad_pre = (gate * grad_mixed).astype(BF16)

    sig_freq, conv_keep, conv_send = forward_call(consts, filt, sig_blocks, F32)
    pre_gate = reduce_ctx(conv_keep, conv_send) + skip * signal.astype(F32)
    mixed = (gate * pre_gate).astype(BF16)

    grad_blocks = gather_ctx(grad_pre)
    cross, back_keep, back_send = backward_call(consts, filt, sig_freq, grad_blocks, F32)
    grad_signal = (reduce_ctx(back_keep, back_send) + skip * grad_pre.astype(F32)).astype(BF16)

    output = project_call(place, out_weight, gather_chan(mixed))
    grad_gating = (grad_mixed * pre_gate).astype(BF16)
    return output, grad_signal, grad_gating, jnp.transpose(cross, (0, 2, 1, 3))


def solution(mesh):
    placed = (
        P("chan", "ctx"),
        P("chan", "ctx"),
        P("chan"),
        P(None, "chan", "ctx", None),
        P(None, "chan"),
        P("ctx", "chan"),
    )
    return jax.shard_map(
        body,
        mesh=mesh,
        in_specs=placed,
        out_specs=(
            P("ctx", "chan"),
            P("chan", "ctx"),
            P("chan", "ctx"),
            P(None, "chan", "ctx", None),
        ),
        check_vma=False,
    )
```

profile of v0, /device:TPU:1, one launch (start us, length us, event | category | flops | bytes accessed | tf_op | source)
XLA Modules:
  0.0 128.4 jit_solution(7346139423485824717)
XLA Ops:
  0.6 7.8 %collective-permute-start = (bf16[256,128]{1,0:T(8,128)(2,1)}, bf16[256,128]{1,0:T(8,128)(2,1)S(1)}, u32[]{:S(2)}, u32[]{:S(2)}) collective-permute-start(bf16[256,128]{1,0:T(8,128)(2,1)} %refs_0_.1), channel_id=1, source_target_pairs={{0,128},{16,144},{32,160},{48,176},{64,192},{80,208},{96,224},{112... | collective-permute-start | bytes 196616 | tf_op jit(solution)/shard_map/ppermute | solution.py:24
  8.5 2.0 %collective-permute-done.refs_1_ = bf16[256,128]{1,0:T(8,128)(2,1)S(1)} collective-permute-done((bf16[256,128]{1,0:T(8,128)(2,1)}, bf16[256,128]{1,0:T(8,128)(2,1)S(1)}, u32[]{:S(2)}, u32[]{:S(2)}) %collective-permute-start) | collective-permute-done | bytes 65568 | tf_op jit(solution)/shard_map/ppermute | solution.py:24
  12.7 2.6 %collective-permute-start.2 = (bf16[2,256,128]{2,1,0:T(8,128)(2,1)S(1)}, bf16[2,256,128]{2,1,0:T(8,128)(2,1)S(1)}, u32[]{:S(2)}, u32[]{:S(2)}) collective-permute-start(bf16[2,256,128]{2,1,0:T(8,128)(2,1)S(1)} %pad_maximum_fusion.1), channel_id=1, source_target_pairs={{0,64},{16,80},{32,96},{48,112},{64,0},{80,16},{96,32},{112,48},{1... | collective-permute-start | bytes 393224 | tf_op jit(solution)/shard_map/ppermute | solution.py:24
  15.3 2.8 %collective-permute-start.4 = (bf16[256,128]{1,0:T(8,128)(2,1)}, bf16[256,128]{1,0:T(8,128)(2,1)S(1)}, u32[]{:S(2)}, u32[]{:S(2)}) collective-permute-start(bf16[256,128]{1,0:T(8,128)(2,1)} %refs_0_.1), channel_id=1, source_target_pairs={{0,16},{16,0},{32,48},{48,32},{64,80},{80,64},{96,112},{112,96},{1... | collective-permute-start | bytes 196616 | tf_op jit(solution)/shard_map/ppermute | solution.py:24
  19.6 3.1 %collective-permute-start.7 = (bf16[2,256,128]{2,1,0:T(8,128)(2,1)S(1)}, bf16[2,256,128]{2,1,0:T(8,128)(2,1)S(1)}, u32[]{:S(2)}, u32[]{:S(2)}) collective-permute-start(bf16[2,256,128]{2,1,0:T(8,128)(2,1)S(1)} %collective-permute-done.2.refs_3_), channel_id=1, source_target_pairs={{0,16},{16,0},{32,48},{48,32},{64,80},{80,64},{96,112},{112,96},{1... | collective-permute-start | bytes 393224 | tf_op jit(solution)/shard_map/ppermute | solution.py:24
  31.0 4.5 %forward_transform.1 = (f32[2,256,256]{2,1,0:T(8,128)S(1)}, f32[8,256,128]{2,1,0:T(8,128)S(1)}, f32[8,256,128]{2,1,0:T(8,128)}) custom-call(f32[64]{0:T(128)S(1)} %dynamic-slice_bitcast_fusion.1.turn_ref, f32[4,128]{1,0:T(4,128)S(1)} %dynamic-slice_bitcast_fusion.twid_ref, f32[256,256]{1,0:T(8,128)S(1)} %copy-done.10, f32[2,2,256,128]{3,2,1,0:T(8,128)S(1)} %bitcast.89, ...), custom_call_target="tpu_custom_call" | custom-call | flops 2000000000 | bytes 4194304 | tf_op jit(solution)/shard_map/forward_transform/pallas_call | solution.py:159
  38.0 2.6 %collective-permute-start.22 = (bf16[4,256,128]{2,1,0:T(8,128)(2,1)S(1)}, bf16[4,256,128]{2,1,0:T(8,128)(2,1)S(1)}, u32[]{:S(2)}, u32[]{:S(2)}) collective-permute-start(bf16[4,256,128]{2,1,0:T(8,128)(2,1)S(1)} %get-tuple-element.20), channel_id=1, source_target_pairs={{0,3},{1,2},{2,1},{3,0},{4,7},{5,6},{6,5},{7,4},{8,11},{9,10},{10,... | collective-permute-start | bytes 786440 | tf_op jit(solution)/shard_map/ppermute | solution.py:24
  41.4 11.4 %collective-permute-done.22 = bf16[4,256,128]{2,1,0:T(8,128)(2,1)S(1)} collective-permute-done((bf16[4,256,128]{2,1,0:T(8,128)(2,1)S(1)}, bf16[4,256,128]{2,1,0:T(8,128)(2,1)S(1)}, u32[]{:S(2)}, u32[]{:S(2)}) %collective-permute-start.22) | collective-permute-done | bytes 262176 | tf_op jit(solution)/shard_map/ppermute | solution.py:24
  56.3 1.8 %collective-permute-start.10 = (bf16[2,256,128]{2,1,0:T(8,128)(2,1)S(1)}, bf16[2,256,128]{2,1,0:T(8,128)(2,1)S(1)}, u32[]{:S(2)}, u32[]{:S(2)}) collective-permute-start(bf16[2,256,128]{2,1,0:T(8,128)(2,1)S(1)} %get-tuple-element.39), channel_id=1, source_target_pairs={{0,32},{16,48},{32,0},{48,16},{64,96},{80,112},{96,64},{112,80},{1... | collective-permute-start | bytes 393224 | tf_op jit(solution)/shard_map/ppermute | solution.py:24
  58.2 2.7 %collective-permute-start.25 = (bf16[256,128]{1,0:T(8,128)(2,1)S(1)}, bf16[256,128]{1,0:T(8,128)(2,1)S(1)}, u32[]{:S(2)}, u32[]{:S(2)}) collective-permute-start(bf16[256,128]{1,0:T(8,128)(2,1)S(1)} %get-tuple-element.44), channel_id=1, source_target_pairs={{0,12},{1,13},{2,14},{3,15},{4,8},{5,9},{6,10},{7,11},{8,4},{9,5},... | collective-permute-start | bytes 196616 | tf_op jit(solution)/shard_map/ppermute | solution.py:24
  63.2 6.0 %collective-permute-start.13 = (bf16[256,128]{1,0:T(8,128)(2,1)S(1)}, bf16[256,128]{1,0:T(8,128)(2,1)S(1)}, u32[]{:S(2)}, u32[]{:S(2)}) collective-permute-start(bf16[256,128]{1,0:T(8,128)(2,1)S(1)} %fusion.16), channel_id=1, source_target_pairs={{0,128},{16,144},{32,160},{48,176},{64,192},{80,208},{96,224},{112... | collective-permute-start | bytes 196616 | tf_op jit(solution)/shard_map/ppermute | solution.py:24
  69.2 2.9 %collective-permute-done.13 = bf16[256,128]{1,0:T(8,128)(2,1)S(1)} collective-permute-done((bf16[256,128]{1,0:T(8,128)(2,1)S(1)}, bf16[256,128]{1,0:T(8,128)(2,1)S(1)}, u32[]{:S(2)}, u32[]{:S(2)}) %collective-permute-start.13) | collective-permute-done | bytes 65568 | tf_op jit(solution)/shard_map/ppermute | solution.py:24
  72.9 4.5 %collective-permute-start.26 = (bf16[256,128]{1,0:T(8,128)(2,1)S(1)}, bf16[256,128]{1,0:T(8,128)(2,1)S(1)}, u32[]{:S(2)}, u32[]{:S(2)}) collective-permute-start(bf16[256,128]{1,0:T(8,128)(2,1)S(1)} %get-tuple-element.35.refs_0_), channel_id=1, source_target_pairs={{0,128},{16,144},{32,160},{48,176},{64,192},{80,208},{96,224},{112... | collective-permute-start | bytes 196616 | tf_op jit(solution)/shard_map/ppermute | solution.py:24
  77.3 2.6 %collective-permute-done.26.refs_1_ = bf16[256,128]{1,0:T(8,128)(2,1)S(1)} collective-permute-done((bf16[256,128]{1,0:T(8,128)(2,1)S(1)}, bf16[256,128]{1,0:T(8,128)(2,1)S(1)}, u32[]{:S(2)}, u32[]{:S(2)}) %collective-permute-start.26) | collective-permute-done | bytes 65568 | tf_op jit(solution)/shard_map/ppermute | solution.py:24
  81.2 2.6 %collective-permute-start.29 = (bf16[2,256,128]{2,1,0:T(8,128)(2,1)S(1)}, bf16[2,256,128]{2,1,0:T(8,128)(2,1)S(1)}, u32[]{:S(2)}, u32[]{:S(2)}) collective-permute-start(bf16[2,256,128]{2,1,0:T(8,128)(2,1)S(1)} %pad_maximum_fusion.2), channel_id=1, source_target_pairs={{0,96},{16,112},{32,64},{48,80},{64,32},{80,48},{96,0},{112,16},{1... | collective-permute-start | bytes 393224 | tf_op jit(solution)/shard_map/ppermute | solution.py:24
  84.1 6.0 %collective-permute-start.32 = (bf16[2,256,128]{2,1,0:T(8,128)(2,1)S(1)}, bf16[2,256,128]{2,1,0:T(8,128)(2,1)S(1)}, u32[]{:S(2)}, u32[]{:S(2)}) collective-permute-start(bf16[2,256,128]{2,1,0:T(8,128)(2,1)S(1)} %collective-permute-done.27.refs_2_), channel_id=1, source_target_pairs={{0,16},{16,0},{32,48},{48,32},{64,80},{80,64},{96,112},{112,96},{1... | collective-permute-start | bytes 393224 | tf_op jit(solution)/shard_map/ppermute | solution.py:24
  94.6 3.6 %backward_transform.1 = (f32[2,2,256,128]{3,2,1,0:T(8,128)S(1)}, f32[8,256,128]{2,1,0:T(8,128)S(1)}, f32[8,256,128]{2,1,0:T(8,128)S(1)}) custom-call(f32[64]{0:T(128)S(1)} %dynamic-slice_bitcast_fusion.1.turn_ref, f32[4,128]{1,0:T(4,128)S(1)} %dynamic-slice_bitcast_fusion.twid_ref, f32[256,256]{1,0:T(8,128)S(1)} %copy-done.11, ...), custom_call_target="tpu_custom_call" | custom-call | flops 2000000000 | bytes 4194304 | tf_op jit(solution)/shard_map/backward_transform/pallas_call | solution.py:177
  98.6 1.9 %collective-permute-start.16 = (bf16[256,128]{1,0:T(8,128)(2,1)S(1)}, bf16[256,128]{1,0:T(8,128)(2,1)S(1)}, u32[]{:S(2)}, u32[]{:S(2)}) collective-permute-start(bf16[256,128]{1,0:T(8,128)(2,1)S(1)} %get-tuple-element.42), channel_id=1, source_target_pairs={{0,12},{1,13},{2,14},{3,15},{4,8},{5,9},{6,10},{7,11},{8,4},{9,5},... | collective-permute-start | bytes 196616 | tf_op jit(solution)/shard_map/ppermute | solution.py:24
  102.4 2.7 %collective-permute-start.38 = (bf16[2,256,128]{2,1,0:T(8,128)(2,1)S(1)}, bf16[2,256,128]{2,1,0:T(8,128)(2,1)S(1)}, u32[]{:S(2)}, u32[]{:S(2)}) collective-permute-start(bf16[2,256,128]{2,1,0:T(8,128)(2,1)S(1)} %get-tuple-element.37), channel_id=1, source_target_pairs={{0,96},{16,112},{32,64},{48,80},{64,32},{80,48},{96,0},{112,16},{1... | collective-permute-start | bytes 393224 | tf_op jit(solution)/shard_map/ppermute | solution.py:24
  109.0 2.5 %collective-permute-start.18 = (bf16[4,256,128]{2,1,0:T(8,128)(2,1)S(1)}, bf16[4,256,128]{2,1,0:T(8,128)(2,1)S(1)}, u32[]{:S(2)}, u32[]{:S(2)}) collective-permute-start(bf16[4,256,128]{2,1,0:T(8,128)(2,1)S(1)} %pad_maximum_fusion.refs_0_), channel_id=1, source_target_pairs={{0,2},{1,3},{2,0},{3,1},{4,6},{5,7},{6,4},{7,5},{8,10},{9,11},{10,... | collective-permute-start | bytes 786440 | tf_op jit(solution)/shard_map/ppermute | solution.py:24
  113.1 4.7 %collective-permute-start.39 = (bf16[256,128]{1,0:T(8,128)(2,1)S(1)}, bf16[256,128]{1,0:T(8,128)(2,1)S(1)}, u32[]{:S(2)}, u32[]{:S(2)}) collective-permute-start(bf16[256,128]{1,0:T(8,128)(2,1)S(1)} %fusion.17), channel_id=1, source_target_pairs={{0,128},{16,144},{32,160},{48,176},{64,192},{80,208},{96,224},{112... | collective-permute-start | bytes 196616 | tf_op jit(solution)/shard_map/ppermute | solution.py:24
  117.7 4.7 %collective-permute-done.18.refs_2_ = bf16[4,256,128]{2,1,0:T(8,128)(2,1)S(1)} collective-permute-done((bf16[4,256,128]{2,1,0:T(8,128)(2,1)S(1)}, bf16[4,256,128]{2,1,0:T(8,128)(2,1)S(1)}, u32[]{:S(2)}, u32[]{:S(2)}) %collective-permute-start.18) | collective-permute-done | bytes 262176 | tf_op jit(solution)/shard_map/ppermute | solution.py:24
  122.5 2.3 %collective-permute-done.19.refs_3_ = bf16[4,256,128]{2,1,0:T(8,128)(2,1)S(1)} collective-permute-done((bf16[4,256,128]{2,1,0:T(8,128)(2,1)S(1)}, bf16[4,256,128]{2,1,0:T(8,128)(2,1)S(1)}, u32[]{:S(2)}, u32[]{:S(2)}) %collective-permute-start.19) | collective-permute-done | bytes 262176 | tf_op jit(solution)/shard_map/ppermute | solution.py:24
  124.8 1.7 %project_output.1 = bf16[128,256]{1,0:T(8,128)(2,1)} custom-call(s32[2]{0:T(128)S(1)} %pad_add_fusion.place_ref, bf16[4096,256]{1,0:T(8,128)(2,1)S(1)} %copy-done, bf16[4,256,128]{2,1,0:T(8,128)(2,1)S(1)} %pad_maximum_fusion.refs_0_, bf16[4,256,128]{2,1,0:T(8,128)(2,1)S(1)} %collective-permute-done.17.refs_1_, ...), custom_call_target="tpu_custom_call" | custom-call | flops 268000000 | bytes 3145728 | tf_op jit(solution)/shard_map/project_output/pallas_call | solution.py:240
  (112 shorter events, 37.6 us)
Async XLA Ops:
  0.6 9.8 %collective-permute-start = (bf16[256,128]{1,0:T(8,128)(2,1)}, bf16[256,128]{1,0:T(8,128)(2,1)S(1)}, u32[]{:S(2)}, u32[]{:S(2)}) collective-permute-start(bf16[256,128]{1,0:T(8,128)(2,1)} %refs_0_.1), channel_id=1, source_target_pairs={{0,128},{16,144},{32,160},{48,176},{64,192},{80,208},{96,224},{112... | collective-permute-start | bytes 196616 | tf_op jit(solution)/shard_map/ppermute | solution.py:24
  15.3 7.4 %collective-permute-start.3 = (bf16[2,256,128]{2,1,0:T(8,128)(2,1)S(1)}, bf16[2,256,128]{2,1,0:T(8,128)(2,1)S(1)}, u32[]{:S(2)}, u32[]{:S(2)}) collective-permute-start(bf16[2,256,128]{2,1,0:T(8,128)(2,1)S(1)} %pad_maximum_fusion.1), channel_id=1, source_target_pairs={{0,96},{16,112},{32,64},{48,80},{64,32},{80,48},{96,0},{112,16},{1... | collective-permute-start | bytes 393224 | tf_op jit(solution)/shard_map/ppermute | solution.py:24
  15.3 11.5 %collective-permute-start.4 = (bf16[256,128]{1,0:T(8,128)(2,1)}, bf16[256,128]{1,0:T(8,128)(2,1)S(1)}, u32[]{:S(2)}, u32[]{:S(2)}) collective-permute-start(bf16[256,128]{1,0:T(8,128)(2,1)} %refs_0_.1), channel_id=1, source_target_pairs={{0,16},{16,0},{32,48},{48,32},{64,80},{80,64},{96,112},{112,96},{1... | collective-permute-start | bytes 196616 | tf_op jit(solution)/shard_map/ppermute | solution.py:24
  18.1 9.3 %collective-permute-start.6 = (bf16[2,256,128]{2,1,0:T(8,128)(2,1)S(1)}, bf16[2,256,128]{2,1,0:T(8,128)(2,1)S(1)}, u32[]{:S(2)}, u32[]{:S(2)}) collective-permute-start(bf16[2,256,128]{2,1,0:T(8,128)(2,1)S(1)} %collective-permute-done.1.refs_2_), channel_id=1, source_target_pairs={{0,16},{16,0},{32,48},{48,32},{64,80},{80,64},{96,112},{112,96},{1... | collective-permute-start | bytes 393224 | tf_op jit(solution)/shard_map/ppermute | solution.py:24
  19.6 7.8 %collective-permute-start.7 = (bf16[2,256,128]{2,1,0:T(8,128)(2,1)S(1)}, bf16[2,256,128]{2,1,0:T(8,128)(2,1)S(1)}, u32[]{:S(2)}, u32[]{:S(2)}) collective-permute-start(bf16[2,256,128]{2,1,0:T(8,128)(2,1)S(1)} %collective-permute-done.2.refs_3_), channel_id=1, source_target_pairs={{0,16},{16,0},{32,48},{48,32},{64,80},{80,64},{96,112},{112,96},{1... | collective-permute-start | bytes 393224 | tf_op jit(solution)/shard_map/ppermute | solution.py:24
  36.2 17.0 %collective-permute-start.9 = (f32[8,256,128]{2,1,0:T(8,128)}, f32[8,256,128]{2,1,0:T(8,128)}, u32[]{:S(2)}, u32[]{:S(2)}) collective-permute-start(f32[8,256,128]{2,1,0:T(8,128)} %get-tuple-element.15), channel_id=1, source_target_pairs={{0,16},{16,0},{32,48},{48,32},{64,80},{80,64},{96,112},{112,96},{1... | collective-permute-start | bytes 3145736 | tf_op jit(solution)/shard_map/ppermute | solution.py:24
  38.0 14.8 %collective-permute-start.22 = (bf16[4,256,128]{2,1,0:T(8,128)(2,1)S(1)}, bf16[4,256,128]{2,1,0:T(8,128)(2,1)S(1)}, u32[]{:S(2)}, u32[]{:S(2)}) collective-permute-start(bf16[4,256,128]{2,1,0:T(8,128)(2,1)S(1)} %get-tuple-element.20), channel_id=1, source_target_pairs={{0,3},{1,2},{2,1},{3,0},{4,7},{5,6},{6,5},{7,4},{8,11},{9,10},{10,... | collective-permute-start | bytes 786440 | tf_op jit(solution)/shard_map/ppermute | solution.py:24
  40.6 12.2 %collective-permute-start.21 = (bf16[4,256,128]{2,1,0:T(8,128)(2,1)S(1)}, bf16[4,256,128]{2,1,0:T(8,128)(2,1)S(1)}, u32[]{:S(2)}, u32[]{:S(2)}) collective-permute-start(bf16[4,256,128]{2,1,0:T(8,128)(2,1)S(1)} %get-tuple-element.19), channel_id=1, source_target_pairs={{0,2},{1,3},{2,0},{3,1},{4,6},{5,7},{6,4},{7,5},{8,10},{9,11},{10,... | collective-permute-start | bytes 786440 | tf_op jit(solution)/shard_map/ppermute | solution.py:24
  41.1 12.0 %collective-permute-start.20 = (bf16[4,256,128]{2,1,0:T(8,128)(2,1)S(1)}, bf16[4,256,128]{2,1,0:T(8,128)(2,1)S(1)}, u32[]{:S(2)}, u32[]{:S(2)}) collective-permute-start(bf16[4,256,128]{2,1,0:T(8,128)(2,1)S(1)} %get-tuple-element.18), channel_id=1, source_target_pairs={{0,1},{1,0},{2,3},{3,2},{4,5},{5,4},{6,7},{7,6},{8,9},{9,8},{10,11... | collective-permute-start | bytes 786440 | tf_op jit(solution)/shard_map/ppermute | solution.py:24
  55.7 7.4 %collective-permute-start.11 = (bf16[2,256,128]{2,1,0:T(8,128)(2,1)S(1)}, bf16[2,256,128]{2,1,0:T(8,128)(2,1)S(1)}, u32[]{:S(2)}, u32[]{:S(2)}) collective-permute-start(bf16[2,256,128]{2,1,0:T(8,128)(2,1)S(1)} %get-tuple-element.41), channel_id=1, source_target_pairs={{0,64},{16,80},{32,96},{48,112},{64,0},{80,16},{96,32},{112,48},{1... | collective-permute-start | bytes 393224 | tf_op jit(solution)/shard_map/ppermute | solution.py:24
  58.2 11.1 %collective-permute-start.25 = (bf16[256,128]{1,0:T(8,128)(2,1)S(1)}, bf16[256,128]{1,0:T(8,128)(2,1)S(1)}, u32[]{:S(2)}, u32[]{:S(2)}) collective-permute-start(bf16[256,128]{1,0:T(8,128)(2,1)S(1)} %get-tuple-element.44), channel_id=1, source_target_pairs={{0,12},{1,13},{2,14},{3,15},{4,8},{5,9},{6,10},{7,11},{8,4},{9,5},... | collective-permute-start | bytes 196616 | tf_op jit(solution)/shard_map/ppermute | solution.py:24
  60.9 8.3 %collective-permute-start.24 = (bf16[256,128]{1,0:T(8,128)(2,1)S(1)}, bf16[256,128]{1,0:T(8,128)(2,1)S(1)}, u32[]{:S(2)}, u32[]{:S(2)}) collective-permute-start(bf16[256,128]{1,0:T(8,128)(2,1)S(1)} %get-tuple-element.45), channel_id=1, source_target_pairs={{0,8},{1,9},{2,10},{3,11},{4,12},{5,13},{6,14},{7,15},{8,0},{9,1},... | collective-permute-start | bytes 196616 | tf_op jit(solution)/shard_map/ppermute | solution.py:24
  61.8 7.4 %collective-permute-start.23 = (bf16[256,128]{1,0:T(8,128)(2,1)S(1)}, bf16[256,128]{1,0:T(8,128)(2,1)S(1)}, u32[]{:S(2)}, u32[]{:S(2)}) collective-permute-start(bf16[256,128]{1,0:T(8,128)(2,1)S(1)} %get-tuple-element.43), channel_id=1, source_target_pairs={{0,4},{1,5},{2,6},{3,7},{4,0},{5,1},{6,2},{7,3},{8,12},{9,13},{10,... | collective-permute-start | bytes 196616 | tf_op jit(solution)/shard_map/ppermute | solution.py:24
  63.2 8.9 %collective-permute-start.13 = (bf16[256,128]{1,0:T(8,128)(2,1)S(1)}, bf16[256,128]{1,0:T(8,128)(2,1)S(1)}, u32[]{:S(2)}, u32[]{:S(2)}) collective-permute-start(bf16[256,128]{1,0:T(8,128)(2,1)S(1)} %fusion.16), channel_id=1, source_target_pairs={{0,128},{16,144},{32,160},{48,176},{64,192},{80,208},{96,224},{112... | collective-permute-start | bytes 196616 | tf_op jit(solution)/shard_map/ppermute | solution.py:24
  80.0 10.1 %collective-permute-start.28 = (bf16[2,256,128]{2,1,0:T(8,128)(2,1)S(1)}, bf16[2,256,128]{2,1,0:T(8,128)(2,1)S(1)}, u32[]{:S(2)}, u32[]{:S(2)}) collective-permute-start(bf16[2,256,128]{2,1,0:T(8,128)(2,1)S(1)} %pad_maximum_fusion.2), channel_id=1, source_target_pairs={{0,64},{16,80},{32,96},{48,112},{64,0},{80,16},{96,32},{112,48},{1... | collective-permute-start | bytes 393224 | tf_op jit(solution)/shard_map/ppermute | solution.py:24
  81.2 10.5 %collective-permute-start.29 = (bf16[2,256,128]{2,1,0:T(8,128)(2,1)S(1)}, bf16[2,256,128]{2,1,0:T(8,128)(2,1)S(1)}, u32[]{:S(2)}, u32[]{:S(2)}) collective-permute-start(bf16[2,256,128]{2,1,0:T(8,128)(2,1)S(1)} %pad_maximum_fusion.2), channel_id=1, source_target_pairs={{0,96},{16,112},{32,64},{48,80},{64,32},{80,48},{96,0},{112,16},{1... | collective-permute-start | bytes 393224 | tf_op jit(solution)/shard_map/ppermute | solution.py:24
  84.1 10.4 %collective-permute-start.32 = (bf16[2,256,128]{2,1,0:T(8,128)(2,1)S(1)}, bf16[2,256,128]{2,1,0:T(8,128)(2,1)S(1)}, u32[]{:S(2)}, u32[]{:S(2)}) collective-permute-start(bf16[2,256,128]{2,1,0:T(8,128)(2,1)S(1)} %collective-permute-done.27.refs_2_), channel_id=1, source_target_pairs={{0,16},{16,0},{32,48},{48,32},{64,80},{80,64},{96,112},{112,96},{1... | collective-permute-start | bytes 393224 | tf_op jit(solution)/shard_map/ppermute | solution.py:24
  102.4 9.0 %collective-permute-start.38 = (bf16[2,256,128]{2,1,0:T(8,128)(2,1)S(1)}, bf16[2,256,128]{2,1,0:T(8,128)(2,1)S(1)}, u32[]{:S(2)}, u32[]{:S(2)}) collective-permute-start(bf16[2,256,128]{2,1,0:T(8,128)(2,1)S(1)} %get-tuple-element.37), channel_id=1, source_target_pairs={{0,96},{16,112},{32,64},{48,80},{64,32},{80,48},{96,0},{112,16},{1... | collective-permute-start | bytes 393224 | tf_op jit(solution)/shard_map/ppermute | solution.py:24
  105.1 7.9 %collective-permute-start.37 = (bf16[2,256,128]{2,1,0:T(8,128)(2,1)S(1)}, bf16[2,256,128]{2,1,0:T(8,128)(2,1)S(1)}, u32[]{:S(2)}, u32[]{:S(2)}) collective-permute-start(bf16[2,256,128]{2,1,0:T(8,128)(2,1)S(1)} %get-tuple-element.38), channel_id=1, source_target_pairs={{0,64},{16,80},{32,96},{48,112},{64,0},{80,16},{96,32},{112,48},{1... | collective-permute-start | bytes 393224 | tf_op jit(solution)/shard_map/ppermute | solution.py:24
  105.1 7.9 %collective-permute-start.36 = (bf16[2,256,128]{2,1,0:T(8,128)(2,1)S(1)}, bf16[2,256,128]{2,1,0:T(8,128)(2,1)S(1)}, u32[]{:S(2)}, u32[]{:S(2)}) collective-permute-start(bf16[2,256,128]{2,1,0:T(8,128)(2,1)S(1)} %get-tuple-element.36), channel_id=1, source_target_pairs={{0,32},{16,48},{32,0},{48,16},{64,96},{80,112},{96,64},{112,80},{1... | collective-permute-start | bytes 393224 | tf_op jit(solution)/shard_map/ppermute | solution.py:24
  107.4 10.3 %collective-permute-start.17 = (bf16[4,256,128]{2,1,0:T(8,128)(2,1)S(1)}, bf16[4,256,128]{2,1,0:T(8,128)(2,1)S(1)}, u32[]{:S(2)}, u32[]{:S(2)}) collective-permute-start(bf16[4,256,128]{2,1,0:T(8,128)(2,1)S(1)} %pad_maximum_fusion.refs_0_), channel_id=1, source_target_pairs={{0,1},{1,0},{2,3},{3,2},{4,5},{5,4},{6,7},{7,6},{8,9},{9,8},{10,11... | collective-permute-start | bytes 786440 | tf_op jit(solution)/shard_map/ppermute | solution.py:24
  109.0 13.5 %collective-permute-start.18 = (bf16[4,256,128]{2,1,0:T(8,128)(2,1)S(1)}, bf16[4,256,128]{2,1,0:T(8,128)(2,1)S(1)}, u32[]{:S(2)}, u32[]{:S(2)}) collective-permute-start(bf16[4,256,128]{2,1,0:T(8,128)(2,1)S(1)} %pad_maximum_fusion.refs_0_), channel_id=1, source_target_pairs={{0,2},{1,3},{2,0},{3,1},{4,6},{5,7},{6,4},{7,5},{8,10},{9,11},{10,... | collective-permute-start | bytes 786440 | tf_op jit(solution)/shard_map/ppermute | solution.py:24
  111.4 13.4 %collective-permute-start.19 = (bf16[4,256,128]{2,1,0:T(8,128)(2,1)S(1)}, bf16[4,256,128]{2,1,0:T(8,128)(2,1)S(1)}, u32[]{:S(2)}, u32[]{:S(2)}) collective-permute-start(bf16[4,256,128]{2,1,0:T(8,128)(2,1)S(1)} %pad_maximum_fusion.refs_0_), channel_id=1, source_target_pairs={{0,3},{1,2},{2,1},{3,0},{4,7},{5,6},{6,5},{7,4},{8,11},{9,10},{10,... | collective-permute-start | bytes 786440 | tf_op jit(solution)/shard_map/ppermute | solution.py:24
  113.1 14.6 %collective-permute-start.39 = (bf16[256,128]{1,0:T(8,128)(2,1)S(1)}, bf16[256,128]{1,0:T(8,128)(2,1)S(1)}, u32[]{:S(2)}, u32[]{:S(2)}) collective-permute-start(bf16[256,128]{1,0:T(8,128)(2,1)S(1)} %fusion.17), channel_id=1, source_target_pairs={{0,128},{16,144},{32,160},{48,176},{64,192},{80,208},{96,224},{112... | collective-permute-start | bytes 196616 | tf_op jit(solution)/shard_map/ppermute | solution.py:24
  (32 other events, 285.5 us)
where the time goes:
time: 129 us; the launch traced here: 128 us
  starting transfers between devices  73.5 us (57%)
  waiting for transfers between devices  30 us (23%)
  Pallas kernels  11 us (9%)
  local copies, waits for them, and re-layouts  8.83 us (7%)
  other arithmetic  4.26 us (3%)
    ppermute x40, starting transfers between devices, swap(): return lax.ppermute(block, axis, [(i, i ^ mask) for i in range(16)])  73.5 us
    ppermute x40, waiting for transfers between devices, swap(): return lax.ppermute(block, axis, [(i, i ^ mask) for i in range(16)])  30 us
    unnamed x34, local copies, waits for them, and re-layouts  7.27 us
    pallas_call x1, Pallas kernels, forward_call(): pl.pallas_call(forward_kernel, out_shape=(jax.ShapeDtypeStruct((2, rows,...  4.49 us
    pallas_call x1, Pallas kernels, backward_call(): pl.pallas_call(backward_kernel, out_shape=(jax.ShapeDtypeStruct((2, 2, ro...  3.56 us
  transfers between devices with their start and end apart: 40, of which 12 were waited for; matrix products, arithmetic and copies ran while one was open for 3% of the time, Pallas kernels for 2%

commit v1 on v0

v1 whole, which is shorter than its diff:
```python
import math

import jax
import jax.numpy as jnp
import numpy as np
from jax import lax
from jax.experimental import pallas as pl
from jax.experimental.pallas import tpu as pltpu
from jax.sharding import PartitionSpec as P

F32 = jnp.float32
BF16 = jnp.bfloat16
VMEM = pl.BlockSpec(memory_space=pltpu.VMEM)
SMEM = pl.BlockSpec(memory_space=pltpu.SMEM)

N_CTX = 16
N_CHAN = 16
SPAN = 128
FULL = 2 * N_CTX * SPAN


def swap(block, axis, mask):
    return lax.ppermute(block, axis, [(i, i ^ mask) for i in range(16)])


def rev4(number):
    return int(f"{number:04b}"[::-1], 2)


def phase(turns, modulus):
    angle = (turns % modulus) * (2.0 * math.pi / modulus)
    return np.cos(angle), np.sin(angle)


def tables():
    ranks = np.arange(N_CTX)
    residues = np.array([[2 * rev4(r ^ 8 * far) + e for far in range(2) for e in range(2)] for r in ranks])
    slots = ranks[:, None] ^ ranks[None, :]
    turn = np.stack(phase(slots[:, None, :] * residues[:, :, None], 32), 1)
    twid = np.stack(phase(residues[:, :, None] * np.arange(SPAN), FULL), 1)
    cos, sin = phase(np.arange(SPAN)[:, None] * np.arange(SPAN), SPAN)
    inner = np.block([[cos, -sin], [sin, cos]]).astype(np.float32)
    high = inner.astype(jnp.bfloat16)
    low = (inner - high.astype(np.float32)).astype(jnp.bfloat16)
    return (
        turn.reshape(N_CTX, 2 * RES * 16).astype(np.float32),
        twid.reshape(N_CTX, 2 * RES, SPAN).astype(np.float32),
        np.stack([high, low]),
    )


def fence(*values):
    return lax.optimization_barrier(values)


def cost(flops, moved):
    return pl.CostEstimate(flops=flops, bytes_accessed=moved, transcendentals=0)


CHUNK = 32
RES = 4


def spread(slot_refs, turn_ref, twid_ref, held_ref):
    rows = held_ref.shape[1]

    def step(n, _):
        at = pl.ds(pl.multiple_of(n * CHUNK, CHUNK), CHUNK)
        acc = [None] * (2 * RES)
        for i, (ref, place) in enumerate(slot_refs):
            x = (ref[at, :] if place is None else ref[place, at, :]).astype(F32)
            for e in range(2 * RES):
                term = x * turn_ref[e * 16 + i]
                acc[e] = term if acc[e] is None else acc[e] + term
        for e in range(RES):
            re, im = acc[e], acc[RES + e]
            cos, sin = twid_ref[pl.ds(e, 1), :], twid_ref[pl.ds(RES + e, 1), :]
            held_ref[e, at, pl.ds(0, SPAN)] = re * cos - im * sin
            held_ref[e, at, pl.ds(SPAN, SPAN)] = -(im * cos + re * sin)
        return _

    lax.fori_loop(0, rows // CHUNK, step, None)


def merge(held_ref, turn_ref, twid_ref, keep_ref, send_ref):
    rows = held_ref.shape[1]

    def step(n, _):
        at = pl.ds(pl.multiple_of(n * CHUNK, CHUNK), CHUNK)
        turned = []
        for e in range(RES):
            re = held_ref[e, at, pl.ds(0, SPAN)] * (1.0 / FULL)
            im = held_ref[e, at, pl.ds(SPAN, SPAN)] * (1.0 / FULL)
            cos, sin = twid_ref[pl.ds(e, 1), :], twid_ref[pl.ds(RES + e, 1), :]
            turned.append((re * cos - im * sin, re * sin + im * cos))
        for i in range(8):
            total = None
            for e in range(RES):
                term = turned[e][0] * turn_ref[e * 16 + i] - turned[e][1] * turn_ref[(RES + e) * 16 + i]
                total = term if total is None else total + term
            out = send_ref if i % 2 else keep_ref
            out[i // 2, at, :] = total
        return _

    lax.fori_loop(0, rows // CHUNK, step, None)


def dft(held, inner_ref, contract):
    high = held.astype(BF16)
    low = (held - high.astype(F32)).astype(BF16)

    def dot(x, y):
        return lax.dot_general(x, y, (((1,), (contract,)), ((), ())), preferred_element_type=F32)

    return dot(high, inner_ref[0]) + (dot(low, inner_ref[0]) + dot(high, inner_ref[1]))


def slot_list(refs):
    slots = {}
    for core in range(2):
        own, far, *pairs = refs[5 * core : 5 * core + 5]
        slots[core] = (own, None)
        slots[8 + core] = (far, None)
        for ky, pair in enumerate(pairs, 1):
            slots[2 * ky + core] = (pair, 0)
            slots[8 + 2 * ky + core] = (pair, 1)
    return [slots[i] for i in range(16)]


def filters(filt_ref, far_ref, e):
    if e < 2:
        return filt_ref[0, e], filt_ref[1, e]
    return far_ref[0, e - 2].astype(F32), far_ref[1, e - 2].astype(F32)


def forward_kernel(turn_ref, twid_ref, inner_ref, filt_ref, far_ref, *refs):
    slot_refs = slot_list(refs[:10])
    freq_ref, keep_ref, send_ref, held_ref = refs[10:]
    spread(slot_refs, turn_ref, twid_ref, held_ref)
    for e in range(RES):
        freq = dft(held_ref[e], inner_ref, 0)
        if e < 2:
            freq_ref[e] = freq
        re, im = freq[:, :SPAN], freq[:, SPAN:]
        filt_re, filt_im = filters(filt_ref, far_ref, e)
        prod = jnp.concatenate([filt_re * re - filt_im * im, filt_re * im + filt_im * re], 1)
        held_ref[e] = dft(prod, inner_ref, 1)
    merge(held_ref, turn_ref, twid_ref, keep_ref, send_ref)


def backward_kernel(turn_ref, twid_ref, inner_ref, filt_ref, far_ref, sig_ref, *refs):
    slot_refs = slot_list(refs[:10])
    cross_ref, keep_ref, send_ref, held_ref = refs[10:]
    spread(slot_refs, turn_ref, twid_ref, held_ref)
    for e in range(RES):
        freq = dft(held_ref[e], inner_ref, 0)
        re, im = freq[:, :SPAN], freq[:, SPAN:]
        if e < 2:
            sig_re, sig_im = sig_ref[e, :, :SPAN], sig_ref[e, :, SPAN:]
            cross_ref[0, e] = (re * sig_re + im * sig_im) * (1.0 / FULL)
            cross_ref[1, e] = (im * sig_re - re * sig_im) * (1.0 / FULL)
        filt_re, filt_im = filters(filt_ref, far_ref, e)
        prod = jnp.concatenate([filt_re * re + filt_im * im, filt_re * im - filt_im * re], 1)
        held_ref[e] = dft(prod, inner_ref, 1)
    merge(held_ref, turn_ref, twid_ref, keep_ref, send_ref)


PARAMS = pltpu.CompilerParams(vmem_limit_bytes=32 * 1024 * 1024)


def transform_call(kernel, name, kept, consts, filt, far, extra, blocks):
    rows = filt.shape[2]
    operands = (*consts, filt, far, *extra, *blocks)
    return pl.pallas_call(
        kernel,
        out_shape=(
            kept,
            jax.ShapeDtypeStruct((4, rows, SPAN), F32),
            jax.ShapeDtypeStruct((4, rows, SPAN), F32),
        ),
        in_specs=[SMEM] + [VMEM] * (len(operands) - 1),
        out_specs=(VMEM,) * 3,
        scratch_shapes=[pltpu.VMEM((RES, rows, 2 * SPAN), F32)],
        compiler_params=PARAMS,
        cost_estimate=cost(2_000_000_000, 4 << 20),
        name=name,
    )(*operands)


def forward_call(consts, filt, far, blocks):
    kept = jax.ShapeDtypeStruct((2, filt.shape[2], 2 * SPAN), F32)
    return transform_call(forward_kernel, "forward_transform", kept, consts, filt, far, (), blocks)


def backward_call(consts, filt, far, sig_freq, blocks):
    kept = jax.ShapeDtypeStruct(filt.shape, F32)
    return transform_call(
        backward_kernel, "backward_transform", kept, consts, filt, far, (sig_freq,), blocks
    )


def fold_kernel(*refs):
    *in_refs, own_ref, a_ref, b_ref, c_ref = refs
    for k, out in enumerate((own_ref, a_ref, b_ref, c_ref)):
        total = in_refs[0][k].astype(F32)
        for ref in in_refs[1:]:
            total = total + ref[k].astype(F32)
        out[...] = total.astype(out.dtype)


def fold_call(*parts):
    block = parts[0].shape[1:]
    return pl.pallas_call(
        fold_kernel,
        out_shape=(jax.ShapeDtypeStruct(block, F32),) + (jax.ShapeDtypeStruct(block, BF16),) * 3,
        in_specs=[VMEM] * len(parts),
        out_specs=(VMEM,) * 4,
        compiler_params=PARAMS,
        cost_estimate=cost(1 << 20, 2 << 20),
        name="fold",
    )(*parts)


def weight_rows(weight_ref, place_ref, kx, kz, rows):
    start = (place_ref[0] ^ kz) * 4 + (place_ref[1] ^ kx)
    return weight_ref[pl.ds(pl.multiple_of(start * rows, rows), rows), :]


def partial_kernel(place_ref, weight_ref, cot_ref, *out_refs):
    rows = out_refs[0].shape[1]
    for kx in (2, 1, 3, 0):
        for kz in range(4):
            out_refs[kx][kz] = lax.dot_general(
                weight_rows(weight_ref, place_ref, kx, kz, rows),
                cot_ref[...],
                (((1,), (1,)), ((), ())),
                preferred_element_type=F32,
            ).astype(BF16)


def partial_call(place, weight, cot):
    rows = weight.shape[0] // N_CHAN
    return pl.pallas_call(
        partial_kernel,
        out_shape=(jax.ShapeDtypeStruct((4, rows, cot.shape[0]), BF16),) * 4,
        in_specs=[SMEM, VMEM, VMEM],
        out_specs=(VMEM,) * 4,
        compiler_params=PARAMS,
        cost_estimate=cost(268_000_000, 3 << 20),
        name="partial_grad_mixed",
    )(place, weight, cot)


def project_kernel(place_ref, weight_ref, *refs):
    out_ref = refs[-1]
    total = None
    for kx in range(4):
        for kz in range(4):
            block = refs[kx][kz]
            term = lax.dot_general(
                block,
                weight_rows(weight_ref, place_ref, kx, kz, block.shape[0]),
                (((0,), (0,)), ((), ())),
                preferred_element_type=F32,
            )
            total = term if total is None else total + term
    out_ref[...] = total.astype(BF16)


def project_call(place, weight, groups):
    return pl.pallas_call(
        project_kernel,
        out_shape=jax.ShapeDtypeStruct((SPAN, weight.shape[1]), BF16),
        in_specs=[SMEM] + [VMEM] * 5,
        out_specs=VMEM,
        compiler_params=PARAMS,
        cost_estimate=cost(268_000_000, 3 << 20),
        name="project_output",
    )(place, weight, *groups)


def gather_ctx(block):
    far = swap(block, "ctx", 8)
    both = jnp.stack([block, far])
    held = [block, far] + [swap(both, "ctx", 2 * ky) for ky in (1, 2, 3)]
    return held + [swap(part, "ctx", 1) for part in held]


def reduce_ctx(keep, send):
    own, *parts = fold_call(keep, swap(send, "ctx", 1))
    for ky, part in enumerate(parts, 1):
        own = own + swap(part, "ctx", 2 * ky).astype(F32)
    return own


def reduce_chan(parts):
    own, *parts = fold_call(parts[0], *[swap(parts[kx], "chan", kx) for kx in (1, 2, 3)])
    for kz, part in enumerate(parts, 1):
        own = own + swap(part, "chan", 4 * kz).astype(F32)
    return own


def gather_chan(block):
    group = jnp.stack([block] + [swap(block, "chan", 4 * kz) for kz in (1, 2, 3)])
    return [group] + [swap(group, "chan", kx) for kx in (1, 2, 3)]


def body(signal, gating, skip_gain, spectrum, out_weight, cotangent):
    ctx = lax.axis_index("ctx")
    chan = lax.axis_index("chan")
    place = jnp.stack([chan // 4, chan % 4]).astype(jnp.int32)
    turn, twid, inner = tables()
    consts = (
        lax.dynamic_index_in_dim(turn, ctx, 0, keepdims=False),
        lax.dynamic_index_in_dim(twid, ctx, 0, keepdims=False),
        jnp.asarray(inner),
    )
    gate = gating.astype(F32)
    skip = skip_gain[:, None]
    filt = jnp.transpose(spectrum, (0, 2, 1, 3))

    sig_far = swap(signal, "ctx", 8)
    far = swap(filt.astype(BF16), "ctx", 8)
    parts = partial_call(place, out_weight, cotangent)
    folded = fold_call(parts[0], *[swap(parts[kx], "chan", kx) for kx in (1, 2, 3)])
    far, folded = fence(far, folded)
    both = jnp.stack([signal, sig_far])
    held = [signal, sig_far] + [swap(both, "ctx", 2 * ky) for ky in (1, 2, 3)]
    sig_blocks = held + [swap(part, "ctx", 1) for part in held]
    grad_mixed, *rest = folded
    for kz, part in enumerate(rest, 1):
        grad_mixed = grad_mixed + swap(part, "chan", 4 * kz).astype(F32)
    grad_pre = (gate * grad_mixed).astype(BF16)
    sig_blocks, grad_pre = fence(sig_blocks, grad_pre)
    grad_far = swap(grad_pre, "ctx", 8)

    sig_freq, conv_keep, conv_send = forward_call(consts, filt, far, sig_blocks)
    conv_keep, conv_send, grad_far = fence(conv_keep, conv_send, grad_far)
    conv = fold_call(conv_keep, swap(conv_send, "ctx", 1))
    conv, grad_far = fence(conv, grad_far)

    conv_own, *rest = conv
    for ky, part in enumerate(rest, 1):
        conv_own = conv_own + swap(part, "ctx", 2 * ky).astype(F32)
    pre_gate = conv_own + skip * signal.astype(F32)
    mixed = (gate * pre_gate).astype(BF16)
    both = jnp.stack([grad_pre, grad_far])
    held = [grad_pre, grad_far] + [swap(both, "ctx", 2 * ky) for ky in (1, 2, 3)]
    mixed, held = fence(mixed, held)

    group = jnp.stack([mixed] + [swap(mixed, "chan", 4 * kz) for kz in (1, 2, 3)])
    grad_blocks = held + [swap(part, "ctx", 1) for part in held]
    cross, back_keep, back_send = backward_call(consts, filt, far, sig_freq, grad_blocks)
    group, back_keep, back_send = fence(group, back_keep, back_send)
    back = fold_call(back_keep, swap(back_send, "ctx", 1))
    groups = [group] + [swap(group, "chan", kx) for kx in (1, 2, 3)]
    back_own, *rest = back
    for ky, part in enumerate(rest, 1):
        back_own = back_own + swap(part, "ctx", 2 * ky).astype(F32)
    grad_signal = (back_own + skip * grad_pre.astype(F32)).astype(BF16)
    output = project_call(place, out_weight, groups)
    grad_gating = (grad_mixed * pre_gate).astype(BF16)
    return output, grad_signal, grad_gating, jnp.transpose(cross, (0, 2, 1, 3))


def solution(mesh):
    placed = (
        P("chan", "ctx"),
        P("chan", "ctx"),
        P("chan"),
        P(None, "chan", "ctx", None),
        P(None, "chan"),
        P("ctx", "chan"),
    )
    return jax.shard_map(
        body,
        mesh=mesh,
        in_specs=placed,
        out_specs=(
            P("ctx", "chan"),
            P("chan", "ctx"),
            P("chan", "ctx"),
            P(None, "chan", "ctx", None),
        ),
        check_vma=False,
    )
```

time: 129 us -> 106 us (0.82)
  starting transfers between devices: 73.5 us -> 58.6 us
  local copies, waits for them, and re-layouts: 8.83 us -> 5.12 us
  waiting for transfers between devices: 30 us -> 27.9 us
  other arithmetic: 4.26 us -> 2.35 us
    ppermute x40 -> x39, starting transfers between devices: 73.5 us -> 58.6 us  [swap(): return lax.ppermute(block, axis, [(i, i ^ mask) for i in range(16)])]
    unnamed x34 -> x19, local copies, waits for them, and re-layouts: 7.27 us -> 3.74 us
    ppermute x40 -> x39, waiting for transfers between devices: 30 us -> 27.9 us  [swap(): return lax.ppermute(block, axis, [(i, i ^ mask) for i in range(16)])]
    add x4 -> x0, other arithmetic: 1.65 us -> none  [the longest x2 1.54 us: reduce_ctx(): keep = keep + swap(send, 'ctx', 1).astype(F32)]
    pallas_call x2 -> x5, Pallas kernels: 8.04 us -> 8.39 us  [the longest x2 8.12 us: transform_call(): pl.pallas_call(kernel, out_shape=(kept, jax.ShapeDtypeStruct((4, rows, SP...]
  transfers between devices with their start and end apart: 40 -> 39, of which waited for: 12 -> 15; matrix products, arithmetic and copies ran while one was open for 3% -> 4% of each run, Pallas kernels for 2% -> 6%
where the time goes in v1:
time: 106 us
  starting transfers between devices  58.6 us (55%)
  waiting for transfers between devices  27.9 us (26%)
  Pallas kernels  11.3 us (11%)
  local copies, waits for them, and re-layouts  5.12 us (5%)
  other arithmetic  2.35 us (2%)
    ppermute x39, starting transfers between devices, swap(): return lax.ppermute(block, axis, [(i, i ^ mask) for i in range(16)])  58.6 us
    ppermute x39, waiting for transfers between devices, swap(): return lax.ppermute(block, axis, [(i, i ^ mask) for i in range(16)])  27.9 us
    pallas_call x2, Pallas kernels, transform_call(): pl.pallas_call(kernel, out_shape=(kept, jax.ShapeDtypeStruct((4, rows, SP...  8.12 us
    unnamed x19, local copies, waits for them, and re-layouts  3.74 us
  transfers between devices with their start and end apart: 39, of which 15 were waited for; matrix products, arithmetic and copies ran while one was open for 4% of the time, Pallas kernels for 6%

profile of v1, /device:TPU:1, one launch (start us, length us, event | category | flops | bytes accessed | tf_op | source)
XLA Modules:
  0.0 106.2 jit_solution(9069686969864116266)
XLA Ops:
  4.4 2.1 %collective-permute-start.1 = (bf16[4,256,128]{2,1,0:T(8,128)(2,1)S(1)}, bf16[4,256,128]{2,1,0:T(8,128)(2,1)S(1)}, u32[]{:S(2)}, u32[]{:S(2)}) collective-permute-start(bf16[4,256,128]{2,1,0:T(8,128)(2,1)S(1)} %get-tuple-element.60), channel_id=1, source_target_pairs={{0,1},{1,0},{2,3},{3,2},{4,5},{5,4},{6,7},{7,6},{8,9},{9,8},{10,11... | collective-permute-start | bytes 786440 | tf_op jit(solution)/shard_map/ppermute | solution.py:23
  6.6 2.5 %collective-permute-start.2 = (bf16[4,256,128]{2,1,0:T(8,128)(2,1)S(1)}, bf16[4,256,128]{2,1,0:T(8,128)(2,1)S(1)}, u32[]{:S(2)}, u32[]{:S(2)}) collective-permute-start(bf16[4,256,128]{2,1,0:T(8,128)(2,1)S(1)} %get-tuple-element.61), channel_id=1, source_target_pairs={{0,2},{1,3},{2,0},{3,1},{4,6},{5,7},{6,4},{7,5},{8,10},{9,11},{10,... | collective-permute-start | bytes 786440 | tf_op jit(solution)/shard_map/ppermute | solution.py:23
  9.0 6.9 %collective-permute-start.4 = (bf16[256,128]{1,0:T(8,128)(2,1)S(1)}, bf16[256,128]{1,0:T(8,128)(2,1)S(1)}, u32[]{:S(2)}, u32[]{:S(2)}) collective-permute-start(bf16[256,128]{1,0:T(8,128)(2,1)S(1)} %copy-done.2), channel_id=1, source_target_pairs={{0,128},{16,144},{32,160},{48,176},{64,192},{80,208},{96,224},{112... | collective-permute-start | bytes 196616 | tf_op jit(solution)/shard_map/ppermute | solution.py:23
  19.6 2.6 %collective-permute-start.6 = (bf16[2,256,128]{2,1,0:T(8,128)(2,1)}, bf16[2,256,128]{2,1,0:T(8,128)(2,1)S(1)}, u32[]{:S(2)}, u32[]{:S(2)}) collective-permute-start(bf16[2,256,128]{2,1,0:T(8,128)(2,1)} %pad_maximum_fusion.1), channel_id=1, source_target_pairs={{0,64},{16,80},{32,96},{48,112},{64,0},{80,16},{96,32},{112,48},{1... | collective-permute-start | bytes 393224 | tf_op jit(solution)/shard_map/ppermute | solution.py:23
  23.8 3.0 %collective-permute-done.3.refs_3_ = bf16[4,256,128]{2,1,0:T(8,128)(2,1)S(1)} collective-permute-done((bf16[4,256,128]{2,1,0:T(8,128)(2,1)S(1)}, bf16[4,256,128]{2,1,0:T(8,128)(2,1)S(1)}, u32[]{:S(2)}, u32[]{:S(2)}) %collective-permute-start.3) | collective-permute-done | bytes 262176 | tf_op jit(solution)/shard_map/ppermute | solution.py:23
  26.9 1.7 %collective-permute-done.far_ref = bf16[2,2,256,128]{3,2,1,0:T(8,128)(2,1)S(1)} collective-permute-done((bf16[2,2,256,128]{3,2,1,0:T(8,128)(2,1)S(1)}, bf16[2,2,256,128]{3,2,1,0:T(8,128)(2,1)S(1)}, u32[]{:S(2)}, u32[]{:S(2)}) %collective-permute-start) | collective-permute-done | bytes 262176 | tf_op jit(solution)/shard_map/ppermute | solution.py:23
  28.6 4.6 %collective-permute-start.13 = (bf16[256,128]{1,0:T(8,128)(2,1)S(1)}, bf16[256,128]{1,0:T(8,128)(2,1)S(1)}, u32[]{:S(2)}, u32[]{:S(2)}) collective-permute-start(bf16[256,128]{1,0:T(8,128)(2,1)S(1)} %get-tuple-element.69), channel_id=1, source_target_pairs={{0,4},{1,5},{2,6},{3,7},{4,0},{5,1},{6,2},{7,3},{8,12},{9,13},{10,... | collective-permute-start | bytes 196616 | tf_op jit(solution)/shard_map/ppermute | solution.py:23
  36.0 2.5 %collective-permute-start.8 = (bf16[256,128]{1,0:T(8,128)(2,1)S(1)}, bf16[256,128]{1,0:T(8,128)(2,1)S(1)}, u32[]{:S(2)}, u32[]{:S(2)}) collective-permute-start(bf16[256,128]{1,0:T(8,128)(2,1)S(1)} %copy-done.2), channel_id=1, source_target_pairs={{0,16},{16,0},{32,48},{48,32},{64,80},{80,64},{96,112},{112,96},{1... | collective-permute-start | bytes 196616 | tf_op jit(solution)/shard_map/ppermute | solution.py:23
  39.1 3.1 %collective-permute-start.11 = (bf16[2,256,128]{2,1,0:T(8,128)(2,1)S(1)}, bf16[2,256,128]{2,1,0:T(8,128)(2,1)S(1)}, u32[]{:S(2)}, u32[]{:S(2)}) collective-permute-start(bf16[2,256,128]{2,1,0:T(8,128)(2,1)S(1)} %collective-permute-done.6.refs_3_), channel_id=1, source_target_pairs={{0,16},{16,0},{32,48},{48,32},{64,80},{80,64},{96,112},{112,96},{1... | collective-permute-start | bytes 393224 | tf_op jit(solution)/shard_map/ppermute | solution.py:23
  43.6 2.7 %collective-permute-start.16 = (bf16[256,128]{1,0:T(8,128)(2,1)S(1)}, bf16[256,128]{1,0:T(8,128)(2,1)S(1)}, u32[]{:S(2)}, u32[]{:S(2)}) collective-permute-start(bf16[256,128]{1,0:T(8,128)(2,1)S(1)} %fusion.refs_0_), channel_id=1, source_target_pairs={{0,128},{16,144},{32,160},{48,176},{64,192},{80,208},{96,224},{112... | collective-permute-start | bytes 196616 | tf_op jit(solution)/shard_map/ppermute | solution.py:23
  46.2 4.0 %forward_transform.1 = (f32[2,256,256]{2,1,0:T(8,128)S(1)}, f32[4,256,128]{2,1,0:T(8,128)S(1)}, f32[4,256,128]{2,1,0:T(8,128)S(1)}) custom-call(f32[128]{0:T(128)S(1)} %dynamic-slice_bitcast_fusion.1.turn_ref, f32[8,128]{1,0:T(8,128)S(1)} %dynamic-slice_bitcast_fusion.twid_ref, bf16[2,256,256]{2,1,0:T(8,128)(2,1)S(1)} %copy-done.4, ...), custom_call_target="tpu_custom_call" | custom-call | flops 2000000000 | bytes 4194304 | tf_op jit(solution)/shard_map/forward_transform/pallas_call | solution.py:174
  55.1 2.6 %collective-permute-start.19 = (bf16[256,128]{1,0:T(8,128)(2,1)S(1)}, bf16[256,128]{1,0:T(8,128)(2,1)S(1)}, u32[]{:S(2)}, u32[]{:S(2)}) collective-permute-start(bf16[256,128]{1,0:T(8,128)(2,1)S(1)} %get-tuple-element.94), channel_id=1, source_target_pairs={{0,64},{16,80},{32,96},{48,112},{64,0},{80,16},{96,32},{112,48},{1... | collective-permute-start | bytes 196616 | tf_op jit(solution)/shard_map/ppermute | solution.py:23
  57.9 3.8 %collective-permute-start.22 = (bf16[2,256,128]{2,1,0:T(8,128)(2,1)S(1)}, bf16[2,256,128]{2,1,0:T(8,128)(2,1)S(1)}, u32[]{:S(2)}, u32[]{:S(2)}) collective-permute-start(bf16[2,256,128]{2,1,0:T(8,128)(2,1)S(1)} %pad_maximum_fusion.2), channel_id=1, source_target_pairs={{0,64},{16,80},{32,96},{48,112},{64,0},{80,16},{96,32},{112,48},{1... | collective-permute-start | bytes 393224 | tf_op jit(solution)/shard_map/ppermute | solution.py:23
  63.0 3.5 %collective-permute-done.22.refs_3_ = bf16[2,256,128]{2,1,0:T(8,128)(2,1)S(1)} collective-permute-done((bf16[2,256,128]{2,1,0:T(8,128)(2,1)S(1)}, bf16[2,256,128]{2,1,0:T(8,128)(2,1)S(1)}, u32[]{:S(2)}, u32[]{:S(2)}) %collective-permute-start.22) | collective-permute-done | bytes 131104 | tf_op jit(solution)/shard_map/ppermute | solution.py:23
  66.5 2.8 %collective-permute-done.23.refs_4_ = bf16[2,256,128]{2,1,0:T(8,128)(2,1)S(1)} collective-permute-done((bf16[2,256,128]{2,1,0:T(8,128)(2,1)S(1)}, bf16[2,256,128]{2,1,0:T(8,128)(2,1)S(1)}, u32[]{:S(2)}, u32[]{:S(2)}) %collective-permute-start.23) | collective-permute-done | bytes 131104 | tf_op jit(solution)/shard_map/ppermute | solution.py:23
  69.3 2.0 %collective-permute-start.24 = (bf16[256,128]{1,0:T(8,128)(2,1)S(1)}, bf16[256,128]{1,0:T(8,128)(2,1)S(1)}, u32[]{:S(2)}, u32[]{:S(2)}) collective-permute-start(bf16[256,128]{1,0:T(8,128)(2,1)S(1)} %fusion.1), channel_id=1, source_target_pairs={{0,4},{1,5},{2,6},{3,7},{4,0},{5,1},{6,2},{7,3},{8,12},{9,13},{10,... | collective-permute-start | bytes 196616 | tf_op jit(solution)/shard_map/ppermute | solution.py:23
  73.4 2.1 %collective-permute-start.29 = (bf16[2,256,128]{2,1,0:T(8,128)(2,1)S(1)}, bf16[2,256,128]{2,1,0:T(8,128)(2,1)S(1)}, u32[]{:S(2)}, u32[]{:S(2)}) collective-permute-start(bf16[2,256,128]{2,1,0:T(8,128)(2,1)S(1)} %collective-permute-done.21.refs_2_), channel_id=1, source_target_pairs={{0,16},{16,0},{32,48},{48,32},{64,80},{80,64},{96,112},{112,96},{1... | collective-permute-start | bytes 393224 | tf_op jit(solution)/shard_map/ppermute | solution.py:23
  76.0 4.2 %collective-permute-start.27 = (bf16[256,128]{1,0:T(8,128)(2,1)S(1)}, bf16[256,128]{1,0:T(8,128)(2,1)S(1)}, u32[]{:S(2)}, u32[]{:S(2)}) collective-permute-start(bf16[256,128]{1,0:T(8,128)(2,1)S(1)} %fusion.refs_0_), channel_id=1, source_target_pairs={{0,16},{16,0},{32,48},{48,32},{64,80},{80,64},{96,112},{112,96},{1... | collective-permute-start | bytes 196616 | tf_op jit(solution)/shard_map/ppermute | solution.py:23
  81.5 4.1 %backward_transform.1 = (f32[2,2,256,128]{3,2,1,0:T(8,128)S(1)}, f32[4,256,128]{2,1,0:T(8,128)S(1)}, f32[4,256,128]{2,1,0:T(8,128)S(1)}) custom-call(f32[128]{0:T(128)S(1)} %dynamic-slice_bitcast_fusion.1.turn_ref, f32[8,128]{1,0:T(8,128)S(1)} %dynamic-slice_bitcast_fusion.twid_ref, bf16[2,256,256]{2,1,0:T(8,128)(2,1)S(1)} %copy-done.4, ...), custom_call_target="tpu_custom_call" | custom-call | flops 2000000000 | bytes 4194304 | tf_op jit(solution)/shard_map/backward_transform/pallas_call | solution.py:174
  85.8 3.9 %collective-permute-start.33 = (bf16[4,256,128]{2,1,0:T(8,128)(2,1)S(1)}, bf16[4,256,128]{2,1,0:T(8,128)(2,1)S(1)}, u32[]{:S(2)}, u32[]{:S(2)}) collective-permute-start(bf16[4,256,128]{2,1,0:T(8,128)(2,1)S(1)} %pad_maximum_fusion.refs_0_), channel_id=1, source_target_pairs={{0,2},{1,3},{2,0},{3,1},{4,6},{5,7},{6,4},{7,5},{8,10},{9,11},{10,... | collective-permute-start | bytes 786440 | tf_op jit(solution)/shard_map/ppermute | solution.py:23
  89.9 1.7 %collective-permute-start.37 = (bf16[256,128]{1,0:T(8,128)(2,1)S(1)}, bf16[256,128]{1,0:T(8,128)(2,1)S(1)}, u32[]{:S(2)}, u32[]{:S(2)}) collective-permute-start(bf16[256,128]{1,0:T(8,128)(2,1)S(1)} %get-tuple-element.111), channel_id=1, source_target_pairs={{0,64},{16,80},{32,96},{48,112},{64,0},{80,16},{96,32},{112,48},{1... | collective-permute-start | bytes 196616 | tf_op jit(solution)/shard_map/ppermute | solution.py:23
  91.7 1.7 %collective-permute-done.32.refs_1_ = bf16[4,256,128]{2,1,0:T(8,128)(2,1)S(1)} collective-permute-done((bf16[4,256,128]{2,1,0:T(8,128)(2,1)S(1)}, bf16[4,256,128]{2,1,0:T(8,128)(2,1)S(1)}, u32[]{:S(2)}, u32[]{:S(2)}) %collective-permute-start.32) | collective-permute-done | bytes 262176 | tf_op jit(solution)/shard_map/ppermute | solution.py:23
  95.2 6.5 %collective-permute-done.33.refs_2_ = bf16[4,256,128]{2,1,0:T(8,128)(2,1)S(1)} collective-permute-done((bf16[4,256,128]{2,1,0:T(8,128)(2,1)S(1)}, bf16[4,256,128]{2,1,0:T(8,128)(2,1)S(1)}, u32[]{:S(2)}, u32[]{:S(2)}) %collective-permute-start.33) | collective-permute-done | bytes 262176 | tf_op jit(solution)/shard_map/ppermute | solution.py:23
  101.7 2.0 %collective-permute-done.34.refs_3_ = bf16[4,256,128]{2,1,0:T(8,128)(2,1)S(1)} collective-permute-done((bf16[4,256,128]{2,1,0:T(8,128)(2,1)S(1)}, bf16[4,256,128]{2,1,0:T(8,128)(2,1)S(1)}, u32[]{:S(2)}, u32[]{:S(2)}) %collective-permute-start.34) | collective-permute-done | bytes 262176 | tf_op jit(solution)/shard_map/ppermute | solution.py:23
  (90 shorter events, 28.5 us)
Async XLA Ops:
  4.4 15.2 %collective-permute-start.1 = (bf16[4,256,128]{2,1,0:T(8,128)(2,1)S(1)}, bf16[4,256,128]{2,1,0:T(8,128)(2,1)S(1)}, u32[]{:S(2)}, u32[]{:S(2)}) collective-permute-start(bf16[4,256,128]{2,1,0:T(8,128)(2,1)S(1)} %get-tuple-element.60), channel_id=1, source_target_pairs={{0,1},{1,0},{2,3},{3,2},{4,5},{5,4},{6,7},{7,6},{8,9},{9,8},{10,11... | collective-permute-start | bytes 786440 | tf_op jit(solution)/shard_map/ppermute | solution.py:23
  6.6 15.7 %collective-permute-start.2 = (bf16[4,256,128]{2,1,0:T(8,128)(2,1)S(1)}, bf16[4,256,128]{2,1,0:T(8,128)(2,1)S(1)}, u32[]{:S(2)}, u32[]{:S(2)}) collective-permute-start(bf16[4,256,128]{2,1,0:T(8,128)(2,1)S(1)} %get-tuple-element.61), channel_id=1, source_target_pairs={{0,2},{1,3},{2,0},{3,1},{4,6},{5,7},{6,4},{7,5},{8,10},{9,11},{10,... | collective-permute-start | bytes 786440 | tf_op jit(solution)/shard_map/ppermute | solution.py:23
  9.0 8.6 %collective-permute-start.4 = (bf16[256,128]{1,0:T(8,128)(2,1)S(1)}, bf16[256,128]{1,0:T(8,128)(2,1)S(1)}, u32[]{:S(2)}, u32[]{:S(2)}) collective-permute-start(bf16[256,128]{1,0:T(8,128)(2,1)S(1)} %copy-done.2), channel_id=1, source_target_pairs={{0,128},{16,144},{32,160},{48,176},{64,192},{80,208},{96,224},{112... | collective-permute-start | bytes 196616 | tf_op jit(solution)/shard_map/ppermute | solution.py:23
  15.9 10.9 %collective-permute-start.3 = (bf16[4,256,128]{2,1,0:T(8,128)(2,1)S(1)}, bf16[4,256,128]{2,1,0:T(8,128)(2,1)S(1)}, u32[]{:S(2)}, u32[]{:S(2)}) collective-permute-start(bf16[4,256,128]{2,1,0:T(8,128)(2,1)S(1)} %get-tuple-element.62), channel_id=1, source_target_pairs={{0,3},{1,2},{2,1},{3,0},{4,7},{5,6},{6,5},{7,4},{8,11},{9,10},{10,... | collective-permute-start | bytes 786440 | tf_op jit(solution)/shard_map/ppermute | solution.py:23
  16.2 12.5 %collective-permute-start = (bf16[2,2,256,128]{3,2,1,0:T(8,128)(2,1)S(1)}, bf16[2,2,256,128]{3,2,1,0:T(8,128)(2,1)S(1)}, u32[]{:S(2)}, u32[]{:S(2)}) collective-permute-start(bf16[2,2,256,128]{3,2,1,0:T(8,128)(2,1)S(1)} %bitcast.28), channel_id=1, source_target_pairs={{0,128},{16,144},{32,160},{48,176},{64,192},{80,208},{96,224},{112... | collective-permute-start | bytes 786440 | tf_op jit(solution)/shard_map/ppermute | solution.py:23
  18.3 15.7 %collective-permute-start.5 = (bf16[2,256,128]{2,1,0:T(8,128)(2,1)}, bf16[2,256,128]{2,1,0:T(8,128)(2,1)S(1)}, u32[]{:S(2)}, u32[]{:S(2)}) collective-permute-start(bf16[2,256,128]{2,1,0:T(8,128)(2,1)} %pad_maximum_fusion.1), channel_id=1, source_target_pairs={{0,32},{16,48},{32,0},{48,16},{64,96},{80,112},{96,64},{112,80},{1... | collective-permute-start | bytes 393224 | tf_op jit(solution)/shard_map/ppermute | solution.py:23
  19.6 16.4 %collective-permute-start.6 = (bf16[2,256,128]{2,1,0:T(8,128)(2,1)}, bf16[2,256,128]{2,1,0:T(8,128)(2,1)S(1)}, u32[]{:S(2)}, u32[]{:S(2)}) collective-permute-start(bf16[2,256,128]{2,1,0:T(8,128)(2,1)} %pad_maximum_fusion.1), channel_id=1, source_target_pairs={{0,64},{16,80},{32,96},{48,112},{64,0},{80,16},{96,32},{112,48},{1... | collective-permute-start | bytes 393224 | tf_op jit(solution)/shard_map/ppermute | solution.py:23
  22.2 16.3 %collective-permute-start.7 = (bf16[2,256,128]{2,1,0:T(8,128)(2,1)}, bf16[2,256,128]{2,1,0:T(8,128)(2,1)S(1)}, u32[]{:S(2)}, u32[]{:S(2)}) collective-permute-start(bf16[2,256,128]{2,1,0:T(8,128)(2,1)} %pad_maximum_fusion.1), channel_id=1, source_target_pairs={{0,96},{16,112},{32,64},{48,80},{64,32},{80,48},{96,0},{112,16},{1... | collective-permute-start | bytes 393224 | tf_op jit(solution)/shard_map/ppermute | solution.py:23
  28.6 10.1 %collective-permute-start.13 = (bf16[256,128]{1,0:T(8,128)(2,1)S(1)}, bf16[256,128]{1,0:T(8,128)(2,1)S(1)}, u32[]{:S(2)}, u32[]{:S(2)}) collective-permute-start(bf16[256,128]{1,0:T(8,128)(2,1)S(1)} %get-tuple-element.69), channel_id=1, source_target_pairs={{0,4},{1,5},{2,6},{3,7},{4,0},{5,1},{6,2},{7,3},{8,12},{9,13},{10,... | collective-permute-start | bytes 196616 | tf_op jit(solution)/shard_map/ppermute | solution.py:23
  34.0 8.2 %collective-permute-start.15 = (bf16[256,128]{1,0:T(8,128)(2,1)S(1)}, bf16[256,128]{1,0:T(8,128)(2,1)S(1)}, u32[]{:S(2)}, u32[]{:S(2)}) collective-permute-start(bf16[256,128]{1,0:T(8,128)(2,1)S(1)} %get-tuple-element.71), channel_id=1, source_target_pairs={{0,12},{1,13},{2,14},{3,15},{4,8},{5,9},{6,10},{7,11},{8,4},{9,5},... | collective-permute-start | bytes 196616 | tf_op jit(solution)/shard_map/ppermute | solution.py:23
  36.0 6.2 %collective-permute-start.8 = (bf16[256,128]{1,0:T(8,128)(2,1)S(1)}, bf16[256,128]{1,0:T(8,128)(2,1)S(1)}, u32[]{:S(2)}, u32[]{:S(2)}) collective-permute-start(bf16[256,128]{1,0:T(8,128)(2,1)S(1)} %copy-done.2), channel_id=1, source_target_pairs={{0,16},{16,0},{32,48},{48,32},{64,80},{80,64},{96,112},{112,96},{1... | collective-permute-start | bytes 196616 | tf_op jit(solution)/shard_map/ppermute | solution.py:23
  43.6 7.4 %collective-permute-start.16 = (bf16[256,128]{1,0:T(8,128)(2,1)S(1)}, bf16[256,128]{1,0:T(8,128)(2,1)S(1)}, u32[]{:S(2)}, u32[]{:S(2)}) collective-permute-start(bf16[256,128]{1,0:T(8,128)(2,1)S(1)} %fusion.refs_0_), channel_id=1, source_target_pairs={{0,128},{16,144},{32,160},{48,176},{64,192},{80,208},{96,224},{112... | collective-permute-start | bytes 196616 | tf_op jit(solution)/shard_map/ppermute | solution.py:23
  53.7 8.0 %collective-permute-start.18 = (bf16[256,128]{1,0:T(8,128)(2,1)S(1)}, bf16[256,128]{1,0:T(8,128)(2,1)S(1)}, u32[]{:S(2)}, u32[]{:S(2)}) collective-permute-start(bf16[256,128]{1,0:T(8,128)(2,1)S(1)} %get-tuple-element.93), channel_id=1, source_target_pairs={{0,32},{16,48},{32,0},{48,16},{64,96},{80,112},{96,64},{112,80},{1... | collective-permute-start | bytes 196616 | tf_op jit(solution)/shard_map/ppermute | solution.py:23
  55.1 6.6 %collective-permute-start.19 = (bf16[256,128]{1,0:T(8,128)(2,1)S(1)}, bf16[256,128]{1,0:T(8,128)(2,1)S(1)}, u32[]{:S(2)}, u32[]{:S(2)}) collective-permute-start(bf16[256,128]{1,0:T(8,128)(2,1)S(1)} %get-tuple-element.94), channel_id=1, source_target_pairs={{0,64},{16,80},{32,96},{48,112},{64,0},{80,16},{96,32},{112,48},{1... | collective-permute-start | bytes 196616 | tf_op jit(solution)/shard_map/ppermute | solution.py:23
  57.9 8.7 %collective-permute-start.22 = (bf16[2,256,128]{2,1,0:T(8,128)(2,1)S(1)}, bf16[2,256,128]{2,1,0:T(8,128)(2,1)S(1)}, u32[]{:S(2)}, u32[]{:S(2)}) collective-permute-start(bf16[2,256,128]{2,1,0:T(8,128)(2,1)S(1)} %pad_maximum_fusion.2), channel_id=1, source_target_pairs={{0,64},{16,80},{32,96},{48,112},{64,0},{80,16},{96,32},{112,48},{1... | collective-permute-start | bytes 393224 | tf_op jit(solution)/shard_map/ppermute | solution.py:23
  61.7 7.6 %collective-permute-start.23 = (bf16[2,256,128]{2,1,0:T(8,128)(2,1)S(1)}, bf16[2,256,128]{2,1,0:T(8,128)(2,1)S(1)}, u32[]{:S(2)}, u32[]{:S(2)}) collective-permute-start(bf16[2,256,128]{2,1,0:T(8,128)(2,1)S(1)} %pad_maximum_fusion.2), channel_id=1, source_target_pairs={{0,96},{16,112},{32,64},{48,80},{64,32},{80,48},{96,0},{112,16},{1... | collective-permute-start | bytes 393224 | tf_op jit(solution)/shard_map/ppermute | solution.py:23
  71.8 8.4 %collective-permute-start.26 = (bf16[256,128]{1,0:T(8,128)(2,1)S(1)}, bf16[256,128]{1,0:T(8,128)(2,1)S(1)}, u32[]{:S(2)}, u32[]{:S(2)}) collective-permute-start(bf16[256,128]{1,0:T(8,128)(2,1)S(1)} %fusion.1), channel_id=1, source_target_pairs={{0,12},{1,13},{2,14},{3,15},{4,8},{5,9},{6,10},{7,11},{8,4},{9,5},... | collective-permute-start | bytes 196616 | tf_op jit(solution)/shard_map/ppermute | solution.py:23
  73.4 8.0 %collective-permute-start.29 = (bf16[2,256,128]{2,1,0:T(8,128)(2,1)S(1)}, bf16[2,256,128]{2,1,0:T(8,128)(2,1)S(1)}, u32[]{:S(2)}, u32[]{:S(2)}) collective-permute-start(bf16[2,256,128]{2,1,0:T(8,128)(2,1)S(1)} %collective-permute-done.21.refs_2_), channel_id=1, source_target_pairs={{0,16},{16,0},{32,48},{48,32},{64,80},{80,64},{96,112},{112,96},{1... | collective-permute-start | bytes 393224 | tf_op jit(solution)/shard_map/ppermute | solution.py:23
  85.8 7.5 %collective-permute-start.32 = (bf16[4,256,128]{2,1,0:T(8,128)(2,1)S(1)}, bf16[4,256,128]{2,1,0:T(8,128)(2,1)S(1)}, u32[]{:S(2)}, u32[]{:S(2)}) collective-permute-start(bf16[4,256,128]{2,1,0:T(8,128)(2,1)S(1)} %pad_maximum_fusion.refs_0_), channel_id=1, source_target_pairs={{0,1},{1,0},{2,3},{3,2},{4,5},{5,4},{6,7},{7,6},{8,9},{9,8},{10,11... | collective-permute-start | bytes 786440 | tf_op jit(solution)/shard_map/ppermute | solution.py:23
  85.8 15.9 %collective-permute-start.33 = (bf16[4,256,128]{2,1,0:T(8,128)(2,1)S(1)}, bf16[4,256,128]{2,1,0:T(8,128)(2,1)S(1)}, u32[]{:S(2)}, u32[]{:S(2)}) collective-permute-start(bf16[4,256,128]{2,1,0:T(8,128)(2,1)S(1)} %pad_maximum_fusion.refs_0_), channel_id=1, source_target_pairs={{0,2},{1,3},{2,0},{3,1},{4,6},{5,7},{6,4},{7,5},{8,10},{9,11},{10,... | collective-permute-start | bytes 786440 | tf_op jit(solution)/shard_map/ppermute | solution.py:23
  89.8 14.0 %collective-permute-start.34 = (bf16[4,256,128]{2,1,0:T(8,128)(2,1)S(1)}, bf16[4,256,128]{2,1,0:T(8,128)(2,1)S(1)}, u32[]{:S(2)}, u32[]{:S(2)}) collective-permute-start(bf16[4,256,128]{2,1,0:T(8,128)(2,1)S(1)} %pad_maximum_fusion.refs_0_), channel_id=1, source_target_pairs={{0,3},{1,2},{2,1},{3,0},{4,7},{5,6},{6,5},{7,4},{8,11},{9,10},{10,... | collective-permute-start | bytes 786440 | tf_op jit(solution)/shard_map/ppermute | solution.py:23
  89.8 15.6 %collective-permute-start.36 = (bf16[256,128]{1,0:T(8,128)(2,1)S(1)}, bf16[256,128]{1,0:T(8,128)(2,1)S(1)}, u32[]{:S(2)}, u32[]{:S(2)}) collective-permute-start(bf16[256,128]{1,0:T(8,128)(2,1)S(1)} %get-tuple-element.110), channel_id=1, source_target_pairs={{0,32},{16,48},{32,0},{48,16},{64,96},{80,112},{96,64},{112,80},{1... | collective-permute-start | bytes 196616 | tf_op jit(solution)/shard_map/ppermute | solution.py:23
  89.9 15.5 %collective-permute-start.37 = (bf16[256,128]{1,0:T(8,128)(2,1)S(1)}, bf16[256,128]{1,0:T(8,128)(2,1)S(1)}, u32[]{:S(2)}, u32[]{:S(2)}) collective-permute-start(bf16[256,128]{1,0:T(8,128)(2,1)S(1)} %get-tuple-element.111), channel_id=1, source_target_pairs={{0,64},{16,80},{32,96},{48,112},{64,0},{80,16},{96,32},{112,48},{1... | collective-permute-start | bytes 196616 | tf_op jit(solution)/shard_map/ppermute | solution.py:23
  93.4 12.0 %collective-permute-start.38 = (bf16[256,128]{1,0:T(8,128)(2,1)S(1)}, bf16[256,128]{1,0:T(8,128)(2,1)S(1)}, u32[]{:S(2)}, u32[]{:S(2)}) collective-permute-start(bf16[256,128]{1,0:T(8,128)(2,1)S(1)} %get-tuple-element.112), channel_id=1, source_target_pairs={{0,96},{16,112},{32,64},{48,80},{64,32},{80,48},{96,0},{112,16},{1... | collective-permute-start | bytes 196616 | tf_op jit(solution)/shard_map/ppermute | solution.py:23
  (23 other events, 199.2 us)

commit v2 on v1

--- a/solution.py
+++ b/solution.py
@@ -322,10 +322,12 @@
     sig_far = swap(signal, "ctx", 8)
     far = swap(filt.astype(BF16), "ctx", 8)
     parts = partial_call(place, out_weight, cotangent)
-    folded = fold_call(parts[0], *[swap(parts[kx], "chan", kx) for kx in (1, 2, 3)])
-    far, folded = fence(far, folded)
+    got = [swap(parts[kx], "chan", kx) for kx in (1, 2, 3)]
+    got[0], got[2], sig_far = fence(got[0], got[2], sig_far)
+    folded = fold_call(parts[0], *got)
     both = jnp.stack([signal, sig_far])
     held = [signal, sig_far] + [swap(both, "ctx", 2 * ky) for ky in (1, 2, 3)]
+    held, far = fence(held, far)
     sig_blocks = held + [swap(part, "ctx", 1) for part in held]
     grad_mixed, *rest = folded
     for kz, part in enumerate(rest, 1):
@@ -337,7 +339,6 @@
     sig_freq, conv_keep, conv_send = forward_call(consts, filt, far, sig_blocks)
     conv_keep, conv_send, grad_far = fence(conv_keep, conv_send, grad_far)
     conv = fold_call(conv_keep, swap(conv_send, "ctx", 1))
-    conv, grad_far = fence(conv, grad_far)
 
     conv_own, *rest = conv
     for ky, part in enumerate(rest, 1):
@@ -346,7 +347,6 @@
     mixed = (gate * pre_gate).astype(BF16)
     both = jnp.stack([grad_pre, grad_far])
     held = [grad_pre, grad_far] + [swap(both, "ctx", 2 * ky) for ky in (1, 2, 3)]
-    mixed, held = fence(mixed, held)
 
     group = jnp.stack([mixed] + [swap(mixed, "chan", 4 * kz) for kz in (1, 2, 3)])
     grad_blocks = held + [swap(part, "ctx", 1) for part in held]

time: 106 us -> 98 us (0.925)
  starting transfers between devices: 58.6 us -> 53.6 us
  waiting for transfers between devices: 27.9 us -> 25.2 us
    ppermute x39, starting transfers between devices: 58.6 us -> 53.6 us  [swap(): return lax.ppermute(block, axis, [(i, i ^ mask) for i in range(16)])]
    ppermute x39, waiting for transfers between devices: 27.9 us -> 25.2 us  [swap(): return lax.ppermute(block, axis, [(i, i ^ mask) for i in range(16)])]
  transfers between devices with their start and end apart: 39 -> 39, of which waited for: 15 -> 12; matrix products, arithmetic and copies ran while one was open for 4% -> 4% of each run, Pallas kernels for 6% -> 10%
where the time goes in v2:
time: 98 us; the launch traced here: 97.8 us
  starting transfers between devices  53.6 us (55%)
  waiting for transfers between devices  25.2 us (26%)
  Pallas kernels  11.3 us (12%)
  local copies, waits for them, and re-layouts  5.12 us (5%)
  other arithmetic  1.69 us (2%)
    ppermute x39, starting transfers between devices, swap(): return lax.ppermute(block, axis, [(i, i ^ mask) for i in range(16)])  53.6 us
    ppermute x39, waiting for transfers between devices, swap(): return lax.ppermute(block, axis, [(i, i ^ mask) for i in range(16)])  25.2 us
    pallas_call x2, Pallas kernels, transform_call(): pl.pallas_call(kernel, out_shape=(kept, jax.ShapeDtypeStruct((4, rows, SP...  8.11 us
    unnamed x19, local copies, waits for them, and re-layouts  3.74 us
  transfers between devices with their start and end apart: 39, of which 12 were waited for; matrix products, arithmetic and copies ran while one was open for 4% of the time, Pallas kernels for 10%

profile of v2, /device:TPU:1, one launch (start us, length us, event | category | flops | bytes accessed | tf_op | source)
XLA Modules:
  0.0 97.8 jit_solution(6505661147911600815)
XLA Ops:
  0.7 1.6 %copy-done = bf16[4096,256]{1,0:T(8,128)(2,1)S(1)} copy-done((bf16[4096,256]{1,0:T(8,128)(2,1)S(1)}, bf16[4096,256]{1,0:T(8,128)(2,1)}, u32[]{:S(2)}) %copy-start) | copy-done | bytes 2097176
  4.4 2.1 %collective-permute-start = (bf16[4,256,128]{2,1,0:T(8,128)(2,1)S(1)}, bf16[4,256,128]{2,1,0:T(8,128)(2,1)S(1)}, u32[]{:S(2)}, u32[]{:S(2)}) collective-permute-start(bf16[4,256,128]{2,1,0:T(8,128)(2,1)S(1)} %get-tuple-element.52), channel_id=1, source_target_pairs={{0,1},{1,0},{2,3},{3,2},{4,5},{5,4},{6,7},{7,6},{8,9},{9,8},{10,11... | collective-permute-start | bytes 786440 | tf_op jit(solution)/shard_map/ppermute | solution.py:23
  6.6 1.8 %collective-permute-start.1 = (bf16[4,256,128]{2,1,0:T(8,128)(2,1)S(1)}, bf16[4,256,128]{2,1,0:T(8,128)(2,1)S(1)}, u32[]{:S(2)}, u32[]{:S(2)}) collective-permute-start(bf16[4,256,128]{2,1,0:T(8,128)(2,1)S(1)} %get-tuple-element.53), channel_id=1, source_target_pairs={{0,3},{1,2},{2,1},{3,0},{4,7},{5,6},{6,5},{7,4},{8,11},{9,10},{10,... | collective-permute-start | bytes 786440 | tf_op jit(solution)/shard_map/ppermute | solution.py:23
  8.4 6.9 %collective-permute-start.2 = (bf16[256,128]{1,0:T(8,128)(2,1)S(1)}, bf16[256,128]{1,0:T(8,128)(2,1)S(1)}, u32[]{:S(2)}, u32[]{:S(2)}) collective-permute-start(bf16[256,128]{1,0:T(8,128)(2,1)S(1)} %copy-done.2), channel_id=1, source_target_pairs={{0,128},{16,144},{32,160},{48,176},{64,192},{80,208},{96,224},{112... | collective-permute-start | bytes 196616 | tf_op jit(solution)/shard_map/ppermute | solution.py:23
  18.4 2.6 %collective-permute-start.4 = (bf16[2,256,128]{2,1,0:T(8,128)(2,1)S(1)}, bf16[2,256,128]{2,1,0:T(8,128)(2,1)S(1)}, u32[]{:S(2)}, u32[]{:S(2)}) collective-permute-start(bf16[2,256,128]{2,1,0:T(8,128)(2,1)S(1)} %pad_maximum_fusion.1), channel_id=1, source_target_pairs={{0,64},{16,80},{32,96},{48,112},{64,0},{80,16},{96,32},{112,48},{1... | collective-permute-start | bytes 393224 | tf_op jit(solution)/shard_map/ppermute | solution.py:23
  23.2 1.7 %collective-permute-start.15 = (bf16[256,128]{1,0:T(8,128)(2,1)S(1)}, bf16[256,128]{1,0:T(8,128)(2,1)S(1)}, u32[]{:S(2)}, u32[]{:S(2)}) collective-permute-start(bf16[256,128]{1,0:T(8,128)(2,1)S(1)} %get-tuple-element.68), channel_id=1, source_target_pairs={{0,12},{1,13},{2,14},{3,15},{4,8},{5,9},{6,10},{7,11},{8,4},{9,5},... | collective-permute-start | bytes 196616 | tf_op jit(solution)/shard_map/ppermute | solution.py:23
  25.0 3.5 %collective-permute-done.6.far_ref = bf16[2,2,256,128]{3,2,1,0:T(8,128)(2,1)S(1)} collective-permute-done((bf16[2,2,256,128]{3,2,1,0:T(8,128)(2,1)S(1)}, bf16[2,2,256,128]{3,2,1,0:T(8,128)(2,1)S(1)}, u32[]{:S(2)}, u32[]{:S(2)}) %collective-permute-start.6) | collective-permute-done | bytes 262176 | tf_op jit(solution)/shard_map/ppermute | solution.py:23
  28.4 5.7 %collective-permute-start.14 = (bf16[256,128]{1,0:T(8,128)(2,1)S(1)}, bf16[256,128]{1,0:T(8,128)(2,1)S(1)}, u32[]{:S(2)}, u32[]{:S(2)}) collective-permute-start(bf16[256,128]{1,0:T(8,128)(2,1)S(1)} %get-tuple-element.67), channel_id=1, source_target_pairs={{0,8},{1,9},{2,10},{3,11},{4,12},{5,13},{6,14},{7,15},{8,0},{9,1},... | collective-permute-start | bytes 196616 | tf_op jit(solution)/shard_map/ppermute | solution.py:23
  34.8 2.5 %collective-permute-start.7 = (bf16[256,128]{1,0:T(8,128)(2,1)S(1)}, bf16[256,128]{1,0:T(8,128)(2,1)S(1)}, u32[]{:S(2)}, u32[]{:S(2)}) collective-permute-start(bf16[256,128]{1,0:T(8,128)(2,1)S(1)} %copy-done.2), channel_id=1, source_target_pairs={{0,16},{16,0},{32,48},{48,32},{64,80},{80,64},{96,112},{112,96},{1... | collective-permute-start | bytes 196616 | tf_op jit(solution)/shard_map/ppermute | solution.py:23
  39.2 1.6 %collective-permute-start.11 = (bf16[2,256,128]{2,1,0:T(8,128)(2,1)S(1)}, bf16[2,256,128]{2,1,0:T(8,128)(2,1)S(1)}, u32[]{:S(2)}, u32[]{:S(2)}) collective-permute-start(bf16[2,256,128]{2,1,0:T(8,128)(2,1)S(1)} %collective-permute-done.5.refs_4_), channel_id=1, source_target_pairs={{0,16},{16,0},{32,48},{48,32},{64,80},{80,64},{96,112},{112,96},{1... | collective-permute-start | bytes 393224 | tf_op jit(solution)/shard_map/ppermute | solution.py:23
  41.8 2.5 %collective-permute-start.16 = (bf16[256,128]{1,0:T(8,128)(2,1)S(1)}, bf16[256,128]{1,0:T(8,128)(2,1)S(1)}, u32[]{:S(2)}, u32[]{:S(2)}) collective-permute-start(bf16[256,128]{1,0:T(8,128)(2,1)S(1)} %fusion.refs_0_), channel_id=1, source_target_pairs={{0,128},{16,144},{32,160},{48,176},{64,192},{80,208},{96,224},{112... | collective-permute-start | bytes 196616 | tf_op jit(solution)/shard_map/ppermute | solution.py:23
  44.3 4.0 %forward_transform.1 = (f32[2,256,256]{2,1,0:T(8,128)S(1)}, f32[4,256,128]{2,1,0:T(8,128)S(1)}, f32[4,256,128]{2,1,0:T(8,128)S(1)}) custom-call(f32[128]{0:T(128)S(1)} %dynamic-slice_bitcast_fusion.1.turn_ref, f32[8,128]{1,0:T(8,128)S(1)} %dynamic-slice_bitcast_fusion.twid_ref, bf16[2,256,256]{2,1,0:T(8,128)(2,1)S(1)} %copy-done.4, ...), custom_call_target="tpu_custom_call" | custom-call | flops 2000000000 | bytes 4194304 | tf_op jit(solution)/shard_map/forward_transform/pallas_call | solution.py:174
  48.9 2.3 %collective-permute-start.17 = (f32[4,256,128]{2,1,0:T(8,128)S(1)}, f32[4,256,128]{2,1,0:T(8,128)S(1)}, u32[]{:S(2)}, u32[]{:S(2)}) collective-permute-start(f32[4,256,128]{2,1,0:T(8,128)S(1)} %get-tuple-element.83), channel_id=1, source_target_pairs={{0,16},{16,0},{32,48},{48,32},{64,80},{80,64},{96,112},{112,96},{1... | collective-permute-start | bytes 1572872 | tf_op jit(solution)/shard_map/ppermute | solution.py:23
  51.7 3.5 %collective-permute-start.25 = (bf16[2,256,128]{2,1,0:T(8,128)(2,1)S(1)}, bf16[2,256,128]{2,1,0:T(8,128)(2,1)S(1)}, u32[]{:S(2)}, u32[]{:S(2)}) collective-permute-start(bf16[2,256,128]{2,1,0:T(8,128)(2,1)S(1)} %pad_maximum_fusion.2), channel_id=1, source_target_pairs={{0,64},{16,80},{32,96},{48,112},{64,0},{80,16},{96,32},{112,48},{1... | collective-permute-start | bytes 393224 | tf_op jit(solution)/shard_map/ppermute | solution.py:23
  55.3 2.8 %collective-permute-start.20 = (bf16[256,128]{1,0:T(8,128)(2,1)S(1)}, bf16[256,128]{1,0:T(8,128)(2,1)S(1)}, u32[]{:S(2)}, u32[]{:S(2)}) collective-permute-start(bf16[256,128]{1,0:T(8,128)(2,1)S(1)} %get-tuple-element.87), channel_id=1, source_target_pairs={{0,96},{16,112},{32,64},{48,80},{64,32},{80,48},{96,0},{112,16},{1... | collective-permute-start | bytes 196616 | tf_op jit(solution)/shard_map/ppermute | solution.py:23
  58.8 3.0 %collective-permute-done.25.refs_3_ = bf16[2,256,128]{2,1,0:T(8,128)(2,1)S(1)} collective-permute-done((bf16[2,256,128]{2,1,0:T(8,128)(2,1)S(1)}, bf16[2,256,128]{2,1,0:T(8,128)(2,1)S(1)}, u32[]{:S(2)}, u32[]{:S(2)}) %collective-permute-start.25) | collective-permute-done | bytes 131104 | tf_op jit(solution)/shard_map/ppermute | solution.py:23
  62.6 3.1 %collective-permute-done.26.refs_4_ = bf16[2,256,128]{2,1,0:T(8,128)(2,1)S(1)} collective-permute-done((bf16[2,256,128]{2,1,0:T(8,128)(2,1)S(1)}, bf16[2,256,128]{2,1,0:T(8,128)(2,1)S(1)}, u32[]{:S(2)}, u32[]{:S(2)}) %collective-permute-start.26) | collective-permute-done | bytes 131104 | tf_op jit(solution)/shard_map/ppermute | solution.py:23
  71.4 1.4 %collective-permute-start.21 = (bf16[256,128]{1,0:T(8,128)(2,1)S(1)}, bf16[256,128]{1,0:T(8,128)(2,1)S(1)}, u32[]{:S(2)}, u32[]{:S(2)}) collective-permute-start(bf16[256,128]{1,0:T(8,128)(2,1)S(1)} %fusion.1), channel_id=1, source_target_pairs={{0,4},{1,5},{2,6},{3,7},{4,0},{5,1},{6,2},{7,3},{8,12},{9,13},{10,... | collective-permute-start | bytes 196616 | tf_op jit(solution)/shard_map/ppermute | solution.py:23
  72.8 4.1 %backward_transform.1 = (f32[2,2,256,128]{3,2,1,0:T(8,128)S(1)}, f32[4,256,128]{2,1,0:T(8,128)S(1)}, f32[4,256,128]{2,1,0:T(8,128)S(1)}) custom-call(f32[128]{0:T(128)S(1)} %dynamic-slice_bitcast_fusion.1.turn_ref, f32[8,128]{1,0:T(8,128)S(1)} %dynamic-slice_bitcast_fusion.twid_ref, bf16[2,256,256]{2,1,0:T(8,128)(2,1)S(1)} %copy-done.4, ...), custom_call_target="tpu_custom_call" | custom-call | flops 2000000000 | bytes 4194304 | tf_op jit(solution)/shard_map/backward_transform/pallas_call | solution.py:174
  79.2 2.1 %collective-permute-start.33 = (bf16[4,256,128]{2,1,0:T(8,128)(2,1)S(1)}, bf16[4,256,128]{2,1,0:T(8,128)(2,1)S(1)}, u32[]{:S(2)}, u32[]{:S(2)}) collective-permute-start(bf16[4,256,128]{2,1,0:T(8,128)(2,1)S(1)} %pad_maximum_fusion.refs_0_), channel_id=1, source_target_pairs={{0,2},{1,3},{2,0},{3,1},{4,6},{5,7},{6,4},{7,5},{8,10},{9,11},{10,... | collective-permute-start | bytes 786440 | tf_op jit(solution)/shard_map/ppermute | solution.py:23
  83.3 3.3 %collective-permute-done.32.refs_1_ = bf16[4,256,128]{2,1,0:T(8,128)(2,1)S(1)} collective-permute-done((bf16[4,256,128]{2,1,0:T(8,128)(2,1)S(1)}, bf16[4,256,128]{2,1,0:T(8,128)(2,1)S(1)}, u32[]{:S(2)}, u32[]{:S(2)}) %collective-permute-start.32) | collective-permute-done | bytes 262176 | tf_op jit(solution)/shard_map/ppermute | solution.py:23
  87.8 5.5 %collective-permute-done.33.refs_2_ = bf16[4,256,128]{2,1,0:T(8,128)(2,1)S(1)} collective-permute-done((bf16[4,256,128]{2,1,0:T(8,128)(2,1)S(1)}, bf16[4,256,128]{2,1,0:T(8,128)(2,1)S(1)}, u32[]{:S(2)}, u32[]{:S(2)}) %collective-permute-start.33) | collective-permute-done | bytes 262176 | tf_op jit(solution)/shard_map/ppermute | solution.py:23
  93.3 2.0 %collective-permute-done.34.refs_3_ = bf16[4,256,128]{2,1,0:T(8,128)(2,1)S(1)} collective-permute-done((bf16[4,256,128]{2,1,0:T(8,128)(2,1)S(1)}, bf16[4,256,128]{2,1,0:T(8,128)(2,1)S(1)}, u32[]{:S(2)}, u32[]{:S(2)}) %collective-permute-start.34) | collective-permute-done | bytes 262176 | tf_op jit(solution)/shard_map/ppermute | solution.py:23
  95.3 1.7 %project_output.1 = bf16[128,256]{1,0:T(8,128)(2,1)} custom-call(s32[2]{0:T(128)S(1)} %pad_add_fusion.place_ref, bf16[4096,256]{1,0:T(8,128)(2,1)S(1)} %copy-done.1, bf16[4,256,128]{2,1,0:T(8,128)(2,1)S(1)} %pad_maximum_fusion.refs_0_, bf16[4,256,128]{2,1,0:T(8,128)(2,1)S(1)} %collective-permute-done.32.refs_1_, ...), custom_call_target="tpu_custom_call" | custom-call | flops 268000000 | bytes 3145728 | tf_op jit(solution)/shard_map/project_output/pallas_call | solution.py:271
  (90 shorter events, 25.6 us)
Async XLA Ops:
  4.4 12.6 %collective-permute-start = (bf16[4,256,128]{2,1,0:T(8,128)(2,1)S(1)}, bf16[4,256,128]{2,1,0:T(8,128)(2,1)S(1)}, u32[]{:S(2)}, u32[]{:S(2)}) collective-permute-start(bf16[4,256,128]{2,1,0:T(8,128)(2,1)S(1)} %get-tuple-element.52), channel_id=1, source_target_pairs={{0,1},{1,0},{2,3},{3,2},{4,5},{5,4},{6,7},{7,6},{8,9},{9,8},{10,11... | collective-permute-start | bytes 786440 | tf_op jit(solution)/shard_map/ppermute | solution.py:23
  6.6 10.5 %collective-permute-start.1 = (bf16[4,256,128]{2,1,0:T(8,128)(2,1)S(1)}, bf16[4,256,128]{2,1,0:T(8,128)(2,1)S(1)}, u32[]{:S(2)}, u32[]{:S(2)}) collective-permute-start(bf16[4,256,128]{2,1,0:T(8,128)(2,1)S(1)} %get-tuple-element.53), channel_id=1, source_target_pairs={{0,3},{1,2},{2,1},{3,0},{4,7},{5,6},{6,5},{7,4},{8,11},{9,10},{10,... | collective-permute-start | bytes 786440 | tf_op jit(solution)/shard_map/ppermute | solution.py:23
  8.4 8.6 %collective-permute-start.2 = (bf16[256,128]{1,0:T(8,128)(2,1)S(1)}, bf16[256,128]{1,0:T(8,128)(2,1)S(1)}, u32[]{:S(2)}, u32[]{:S(2)}) collective-permute-start(bf16[256,128]{1,0:T(8,128)(2,1)S(1)} %copy-done.2), channel_id=1, source_target_pairs={{0,128},{16,144},{32,160},{48,176},{64,192},{80,208},{96,224},{112... | collective-permute-start | bytes 196616 | tf_op jit(solution)/shard_map/ppermute | solution.py:23
  15.3 7.8 %collective-permute-start.12 = (bf16[4,256,128]{2,1,0:T(8,128)(2,1)S(1)}, bf16[4,256,128]{2,1,0:T(8,128)(2,1)S(1)}, u32[]{:S(2)}, u32[]{:S(2)}) collective-permute-start(bf16[4,256,128]{2,1,0:T(8,128)(2,1)S(1)} %get-tuple-element.63), channel_id=1, source_target_pairs={{0,2},{1,3},{2,0},{3,1},{4,6},{5,7},{6,4},{7,5},{8,10},{9,11},{10,... | collective-permute-start | bytes 786440 | tf_op jit(solution)/shard_map/ppermute | solution.py:23
  16.0 12.4 %collective-permute-start.6 = (bf16[2,2,256,128]{3,2,1,0:T(8,128)(2,1)S(1)}, bf16[2,2,256,128]{3,2,1,0:T(8,128)(2,1)S(1)}, u32[]{:S(2)}, u32[]{:S(2)}) collective-permute-start(bf16[2,2,256,128]{3,2,1,0:T(8,128)(2,1)S(1)} %bitcast.28), channel_id=1, source_target_pairs={{0,128},{16,144},{32,160},{48,176},{64,192},{80,208},{96,224},{112... | collective-permute-start | bytes 786440 | tf_op jit(solution)/shard_map/ppermute | solution.py:23
  17.0 17.1 %collective-permute-start.3 = (bf16[2,256,128]{2,1,0:T(8,128)(2,1)S(1)}, bf16[2,256,128]{2,1,0:T(8,128)(2,1)S(1)}, u32[]{:S(2)}, u32[]{:S(2)}) collective-permute-start(bf16[2,256,128]{2,1,0:T(8,128)(2,1)S(1)} %pad_maximum_fusion.1), channel_id=1, source_target_pairs={{0,32},{16,48},{32,0},{48,16},{64,96},{80,112},{96,64},{112,80},{1... | collective-permute-start | bytes 393224 | tf_op jit(solution)/shard_map/ppermute | solution.py:23
  18.4 16.4 %collective-permute-start.4 = (bf16[2,256,128]{2,1,0:T(8,128)(2,1)S(1)}, bf16[2,256,128]{2,1,0:T(8,128)(2,1)S(1)}, u32[]{:S(2)}, u32[]{:S(2)}) collective-permute-start(bf16[2,256,128]{2,1,0:T(8,128)(2,1)S(1)} %pad_maximum_fusion.1), channel_id=1, source_target_pairs={{0,64},{16,80},{32,96},{48,112},{64,0},{80,16},{96,32},{112,48},{1... | collective-permute-start | bytes 393224 | tf_op jit(solution)/shard_map/ppermute | solution.py:23
  21.0 13.8 %collective-permute-start.5 = (bf16[2,256,128]{2,1,0:T(8,128)(2,1)S(1)}, bf16[2,256,128]{2,1,0:T(8,128)(2,1)S(1)}, u32[]{:S(2)}, u32[]{:S(2)}) collective-permute-start(bf16[2,256,128]{2,1,0:T(8,128)(2,1)S(1)} %pad_maximum_fusion.1), channel_id=1, source_target_pairs={{0,96},{16,112},{32,64},{48,80},{64,32},{80,48},{96,0},{112,16},{1... | collective-permute-start | bytes 393224 | tf_op jit(solution)/shard_map/ppermute | solution.py:23
  23.2 14.2 %collective-permute-start.15 = (bf16[256,128]{1,0:T(8,128)(2,1)S(1)}, bf16[256,128]{1,0:T(8,128)(2,1)S(1)}, u32[]{:S(2)}, u32[]{:S(2)}) collective-permute-start(bf16[256,128]{1,0:T(8,128)(2,1)S(1)} %get-tuple-element.68), channel_id=1, source_target_pairs={{0,12},{1,13},{2,14},{3,15},{4,8},{5,9},{6,10},{7,11},{8,4},{9,5},... | collective-permute-start | bytes 196616 | tf_op jit(solution)/shard_map/ppermute | solution.py:23
  28.4 9.4 %collective-permute-start.14 = (bf16[256,128]{1,0:T(8,128)(2,1)S(1)}, bf16[256,128]{1,0:T(8,128)(2,1)S(1)}, u32[]{:S(2)}, u32[]{:S(2)}) collective-permute-start(bf16[256,128]{1,0:T(8,128)(2,1)S(1)} %get-tuple-element.67), channel_id=1, source_target_pairs={{0,8},{1,9},{2,10},{3,11},{4,12},{5,13},{6,14},{7,15},{8,0},{9,1},... | collective-permute-start | bytes 196616 | tf_op jit(solution)/shard_map/ppermute | solution.py:23
  51.7 10.1 %collective-permute-start.25 = (bf16[2,256,128]{2,1,0:T(8,128)(2,1)S(1)}, bf16[2,256,128]{2,1,0:T(8,128)(2,1)S(1)}, u32[]{:S(2)}, u32[]{:S(2)}) collective-permute-start(bf16[2,256,128]{2,1,0:T(8,128)(2,1)S(1)} %pad_maximum_fusion.2), channel_id=1, source_target_pairs={{0,64},{16,80},{32,96},{48,112},{64,0},{80,16},{96,32},{112,48},{1... | collective-permute-start | bytes 393224 | tf_op jit(solution)/shard_map/ppermute | solution.py:23
  55.2 10.5 %collective-permute-start.26 = (bf16[2,256,128]{2,1,0:T(8,128)(2,1)S(1)}, bf16[2,256,128]{2,1,0:T(8,128)(2,1)S(1)}, u32[]{:S(2)}, u32[]{:S(2)}) collective-permute-start(bf16[2,256,128]{2,1,0:T(8,128)(2,1)S(1)} %pad_maximum_fusion.2), channel_id=1, source_target_pairs={{0,96},{16,112},{32,64},{48,80},{64,32},{80,48},{96,0},{112,16},{1... | collective-permute-start | bytes 393224 | tf_op jit(solution)/shard_map/ppermute | solution.py:23
  55.3 11.8 %collective-permute-start.20 = (bf16[256,128]{1,0:T(8,128)(2,1)S(1)}, bf16[256,128]{1,0:T(8,128)(2,1)S(1)}, u32[]{:S(2)}, u32[]{:S(2)}) collective-permute-start(bf16[256,128]{1,0:T(8,128)(2,1)S(1)} %get-tuple-element.87), channel_id=1, source_target_pairs={{0,96},{16,112},{32,64},{48,80},{64,32},{80,48},{96,0},{112,16},{1... | collective-permute-start | bytes 196616 | tf_op jit(solution)/shard_map/ppermute | solution.py:23
  58.1 9.8 %collective-permute-start.19 = (bf16[256,128]{1,0:T(8,128)(2,1)S(1)}, bf16[256,128]{1,0:T(8,128)(2,1)S(1)}, u32[]{:S(2)}, u32[]{:S(2)}) collective-permute-start(bf16[256,128]{1,0:T(8,128)(2,1)S(1)} %get-tuple-element.86), channel_id=1, source_target_pairs={{0,64},{16,80},{32,96},{48,112},{64,0},{80,16},{96,32},{112,48},{1... | collective-permute-start | bytes 196616 | tf_op jit(solution)/shard_map/ppermute | solution.py:23
  58.1 9.8 %collective-permute-start.18 = (bf16[256,128]{1,0:T(8,128)(2,1)S(1)}, bf16[256,128]{1,0:T(8,128)(2,1)S(1)}, u32[]{:S(2)}, u32[]{:S(2)}) collective-permute-start(bf16[256,128]{1,0:T(8,128)(2,1)S(1)} %get-tuple-element.85), channel_id=1, source_target_pairs={{0,32},{16,48},{32,0},{48,16},{64,96},{80,112},{96,64},{112,80},{1... | collective-permute-start | bytes 196616 | tf_op jit(solution)/shard_map/ppermute | solution.py:23
  61.7 7.4 %collective-permute-start.27 = (bf16[256,128]{1,0:T(8,128)(2,1)S(1)}, bf16[256,128]{1,0:T(8,128)(2,1)S(1)}, u32[]{:S(2)}, u32[]{:S(2)}) collective-permute-start(bf16[256,128]{1,0:T(8,128)(2,1)S(1)} %fusion.refs_0_), channel_id=1, source_target_pairs={{0,16},{16,0},{32,48},{48,32},{64,80},{80,64},{96,112},{112,96},{1... | collective-permute-start | bytes 196616 | tf_op jit(solution)/shard_map/ppermute | solution.py:23
  69.1 7.8 %collective-permute-start.23 = (bf16[256,128]{1,0:T(8,128)(2,1)S(1)}, bf16[256,128]{1,0:T(8,128)(2,1)S(1)}, u32[]{:S(2)}, u32[]{:S(2)}) collective-permute-start(bf16[256,128]{1,0:T(8,128)(2,1)S(1)} %fusion.1), channel_id=1, source_target_pairs={{0,12},{1,13},{2,14},{3,15},{4,8},{5,9},{6,10},{7,11},{8,4},{9,5},... | collective-permute-start | bytes 196616 | tf_op jit(solution)/shard_map/ppermute | solution.py:23
  70.0 7.8 %collective-permute-start.22 = (bf16[256,128]{1,0:T(8,128)(2,1)S(1)}, bf16[256,128]{1,0:T(8,128)(2,1)S(1)}, u32[]{:S(2)}, u32[]{:S(2)}) collective-permute-start(bf16[256,128]{1,0:T(8,128)(2,1)S(1)} %fusion.1), channel_id=1, source_target_pairs={{0,8},{1,9},{2,10},{3,11},{4,12},{5,13},{6,14},{7,15},{8,0},{9,1},... | collective-permute-start | bytes 196616 | tf_op jit(solution)/shard_map/ppermute | solution.py:23
  78.8 7.9 %collective-permute-start.32 = (bf16[4,256,128]{2,1,0:T(8,128)(2,1)S(1)}, bf16[4,256,128]{2,1,0:T(8,128)(2,1)S(1)}, u32[]{:S(2)}, u32[]{:S(2)}) collective-permute-start(bf16[4,256,128]{2,1,0:T(8,128)(2,1)S(1)} %pad_maximum_fusion.refs_0_), channel_id=1, source_target_pairs={{0,1},{1,0},{2,3},{3,2},{4,5},{5,4},{6,7},{7,6},{8,9},{9,8},{10,11... | collective-permute-start | bytes 786440 | tf_op jit(solution)/shard_map/ppermute | solution.py:23
  79.2 14.1 %collective-permute-start.33 = (bf16[4,256,128]{2,1,0:T(8,128)(2,1)S(1)}, bf16[4,256,128]{2,1,0:T(8,128)(2,1)S(1)}, u32[]{:S(2)}, u32[]{:S(2)}) collective-permute-start(bf16[4,256,128]{2,1,0:T(8,128)(2,1)S(1)} %pad_maximum_fusion.refs_0_), channel_id=1, source_target_pairs={{0,2},{1,3},{2,0},{3,1},{4,6},{5,7},{6,4},{7,5},{8,10},{9,11},{10,... | collective-permute-start | bytes 786440 | tf_op jit(solution)/shard_map/ppermute | solution.py:23
  81.3 14.0 %collective-permute-start.34 = (bf16[4,256,128]{2,1,0:T(8,128)(2,1)S(1)}, bf16[4,256,128]{2,1,0:T(8,128)(2,1)S(1)}, u32[]{:S(2)}, u32[]{:S(2)}) collective-permute-start(bf16[4,256,128]{2,1,0:T(8,128)(2,1)S(1)} %pad_maximum_fusion.refs_0_), channel_id=1, source_target_pairs={{0,3},{1,2},{2,1},{3,0},{4,7},{5,6},{6,5},{7,4},{8,11},{9,10},{10,... | collective-permute-start | bytes 786440 | tf_op jit(solution)/shard_map/ppermute | solution.py:23
  82.7 14.3 %collective-permute-start.38 = (bf16[256,128]{1,0:T(8,128)(2,1)S(1)}, bf16[256,128]{1,0:T(8,128)(2,1)S(1)}, u32[]{:S(2)}, u32[]{:S(2)}) collective-permute-start(bf16[256,128]{1,0:T(8,128)(2,1)S(1)} %get-tuple-element.98), channel_id=1, source_target_pairs={{0,96},{16,112},{32,64},{48,80},{64,32},{80,48},{96,0},{112,16},{1... | collective-permute-start | bytes 196616 | tf_op jit(solution)/shard_map/ppermute | solution.py:23
  82.8 14.2 %collective-permute-start.37 = (bf16[256,128]{1,0:T(8,128)(2,1)S(1)}, bf16[256,128]{1,0:T(8,128)(2,1)S(1)}, u32[]{:S(2)}, u32[]{:S(2)}) collective-permute-start(bf16[256,128]{1,0:T(8,128)(2,1)S(1)} %get-tuple-element.97), channel_id=1, source_target_pairs={{0,64},{16,80},{32,96},{48,112},{64,0},{80,16},{96,32},{112,48},{1... | collective-permute-start | bytes 196616 | tf_op jit(solution)/shard_map/ppermute | solution.py:23
  86.6 10.4 %collective-permute-start.36 = (bf16[256,128]{1,0:T(8,128)(2,1)S(1)}, bf16[256,128]{1,0:T(8,128)(2,1)S(1)}, u32[]{:S(2)}, u32[]{:S(2)}) collective-permute-start(bf16[256,128]{1,0:T(8,128)(2,1)S(1)} %get-tuple-element.96), channel_id=1, source_target_pairs={{0,32},{16,48},{32,0},{48,16},{64,96},{80,112},{96,64},{112,80},{1... | collective-permute-start | bytes 196616 | tf_op jit(solution)/shard_map/ppermute | solution.py:23
  (23 other events, 213.0 us)

commit v3 on v2

--- a/solution.py
+++ b/solution.py
@@ -358,9 +358,11 @@
     for ky, part in enumerate(rest, 1):
         back_own = back_own + swap(part, "ctx", 2 * ky).astype(F32)
     grad_signal = (back_own + skip * grad_pre.astype(F32)).astype(BF16)
+    grad_spectrum = jnp.transpose(cross, (0, 2, 1, 3))
+    groups, grad_signal, grad_spectrum = fence(groups, grad_signal, grad_spectrum)
     output = project_call(place, out_weight, groups)
     grad_gating = (grad_mixed * pre_gate).astype(BF16)
-    return output, grad_signal, grad_gating, jnp.transpose(cross, (0, 2, 1, 3))
+    return output, grad_signal, grad_gating, grad_spectrum
 
 
 def solution(mesh):

time: 98 us -> 103 us (1.051)
  starting transfers between devices: 53.6 us -> 56.2 us
  waiting for transfers between devices: 25.2 us -> 27.4 us
    ppermute x39, starting transfers between devices: 53.6 us -> 56.2 us  [swap(): return lax.ppermute(block, axis, [(i, i ^ mask) for i in range(16)])]
    ppermute x39, waiting for transfers between devices: 25.2 us -> 27.4 us  [swap(): return lax.ppermute(block, axis, [(i, i ^ mask) for i in range(16)])]
  transfers between devices with their start and end apart: 39 -> 39, of which waited for: 12 -> 14; matrix products, arithmetic and copies ran while one was open for 4% -> 3% of each run, Pallas kernels for 10% -> 8%
where the time goes in v3:
time: 103 us
  starting transfers between devices  56.2 us (55%)
  waiting for transfers between devices  27.4 us (27%)
  Pallas kernels  11.3 us (11%)
  local copies, waits for them, and re-layouts  5.12 us (5%)
  other arithmetic  1.69 us (2%)
    ppermute x39, starting transfers between devices, swap(): return lax.ppermute(block, axis, [(i, i ^ mask) for i in range(16)])  56.2 us
    ppermute x39, waiting for transfers between devices, swap(): return lax.ppermute(block, axis, [(i, i ^ mask) for i in range(16)])  27.4 us
    pallas_call x2, Pallas kernels, transform_call(): pl.pallas_call(kernel, out_shape=(kept, jax.ShapeDtypeStruct((4, rows, SP...  8.11 us
    unnamed x19, local copies, waits for them, and re-layouts  3.74 us
  transfers between devices with their start and end apart: 39, of which 14 were waited for; matrix products, arithmetic and copies ran while one was open for 3% of the time, Pallas kernels for 8%

profile of v3, /device:TPU:1, one launch (start us, length us, event | category | flops | bytes accessed | tf_op | source)
XLA Modules:
  0.0 102.6 jit_solution(16195876759489983722)
XLA Ops:
  0.7 1.6 %copy-done = bf16[4096,256]{1,0:T(8,128)(2,1)S(1)} copy-done((bf16[4096,256]{1,0:T(8,128)(2,1)S(1)}, bf16[4096,256]{1,0:T(8,128)(2,1)}, u32[]{:S(2)}) %copy-start) | copy-done | bytes 2097176
  4.4 2.1 %collective-permute-start = (bf16[4,256,128]{2,1,0:T(8,128)(2,1)S(1)}, bf16[4,256,128]{2,1,0:T(8,128)(2,1)S(1)}, u32[]{:S(2)}, u32[]{:S(2)}) collective-permute-start(bf16[4,256,128]{2,1,0:T(8,128)(2,1)S(1)} %get-tuple-element.58), channel_id=1, source_target_pairs={{0,1},{1,0},{2,3},{3,2},{4,5},{5,4},{6,7},{7,6},{8,9},{9,8},{10,11... | collective-permute-start | bytes 786440 | tf_op jit(solution)/shard_map/ppermute | solution.py:23
  6.6 1.8 %collective-permute-start.1 = (bf16[4,256,128]{2,1,0:T(8,128)(2,1)S(1)}, bf16[4,256,128]{2,1,0:T(8,128)(2,1)S(1)}, u32[]{:S(2)}, u32[]{:S(2)}) collective-permute-start(bf16[4,256,128]{2,1,0:T(8,128)(2,1)S(1)} %get-tuple-element.59), channel_id=1, source_target_pairs={{0,3},{1,2},{2,1},{3,0},{4,7},{5,6},{6,5},{7,4},{8,11},{9,10},{10,... | collective-permute-start | bytes 786440 | tf_op jit(solution)/shard_map/ppermute | solution.py:23
  8.4 6.9 %collective-permute-start.2 = (bf16[256,128]{1,0:T(8,128)(2,1)S(1)}, bf16[256,128]{1,0:T(8,128)(2,1)S(1)}, u32[]{:S(2)}, u32[]{:S(2)}) collective-permute-start(bf16[256,128]{1,0:T(8,128)(2,1)S(1)} %copy-done.2), channel_id=1, source_target_pairs={{0,128},{16,144},{32,160},{48,176},{64,192},{80,208},{96,224},{112... | collective-permute-start | bytes 196616 | tf_op jit(solution)/shard_map/ppermute | solution.py:23
  18.4 2.6 %collective-permute-start.4 = (bf16[2,256,128]{2,1,0:T(8,128)(2,1)S(1)}, bf16[2,256,128]{2,1,0:T(8,128)(2,1)S(1)}, u32[]{:S(2)}, u32[]{:S(2)}) collective-permute-start(bf16[2,256,128]{2,1,0:T(8,128)(2,1)S(1)} %pad_maximum_fusion.1), channel_id=1, source_target_pairs={{0,64},{16,80},{32,96},{48,112},{64,0},{80,16},{96,32},{112,48},{1... | collective-permute-start | bytes 393224 | tf_op jit(solution)/shard_map/ppermute | solution.py:23
  23.2 1.7 %collective-permute-start.15 = (bf16[256,128]{1,0:T(8,128)(2,1)S(1)}, bf16[256,128]{1,0:T(8,128)(2,1)S(1)}, u32[]{:S(2)}, u32[]{:S(2)}) collective-permute-start(bf16[256,128]{1,0:T(8,128)(2,1)S(1)} %get-tuple-element.74), channel_id=1, source_target_pairs={{0,12},{1,13},{2,14},{3,15},{4,8},{5,9},{6,10},{7,11},{8,4},{9,5},... | collective-permute-start | bytes 196616 | tf_op jit(solution)/shard_map/ppermute | solution.py:23
  25.0 3.5 %collective-permute-done.6.far_ref = bf16[2,2,256,128]{3,2,1,0:T(8,128)(2,1)S(1)} collective-permute-done((bf16[2,2,256,128]{3,2,1,0:T(8,128)(2,1)S(1)}, bf16[2,2,256,128]{3,2,1,0:T(8,128)(2,1)S(1)}, u32[]{:S(2)}, u32[]{:S(2)}) %collective-permute-start.6) | collective-permute-done | bytes 262176 | tf_op jit(solution)/shard_map/ppermute | solution.py:23
  28.4 5.7 %collective-permute-start.14 = (bf16[256,128]{1,0:T(8,128)(2,1)S(1)}, bf16[256,128]{1,0:T(8,128)(2,1)S(1)}, u32[]{:S(2)}, u32[]{:S(2)}) collective-permute-start(bf16[256,128]{1,0:T(8,128)(2,1)S(1)} %get-tuple-element.73), channel_id=1, source_target_pairs={{0,8},{1,9},{2,10},{3,11},{4,12},{5,13},{6,14},{7,15},{8,0},{9,1},... | collective-permute-start | bytes 196616 | tf_op jit(solution)/shard_map/ppermute | solution.py:23
  34.8 2.5 %collective-permute-start.7 = (bf16[256,128]{1,0:T(8,128)(2,1)S(1)}, bf16[256,128]{1,0:T(8,128)(2,1)S(1)}, u32[]{:S(2)}, u32[]{:S(2)}) collective-permute-start(bf16[256,128]{1,0:T(8,128)(2,1)S(1)} %copy-done.2), channel_id=1, source_target_pairs={{0,16},{16,0},{32,48},{48,32},{64,80},{80,64},{96,112},{112,96},{1... | collective-permute-start | bytes 196616 | tf_op jit(solution)/shard_map/ppermute | solution.py:23
  39.2 1.6 %collective-permute-start.11 = (bf16[2,256,128]{2,1,0:T(8,128)(2,1)S(1)}, bf16[2,256,128]{2,1,0:T(8,128)(2,1)S(1)}, u32[]{:S(2)}, u32[]{:S(2)}) collective-permute-start(bf16[2,256,128]{2,1,0:T(8,128)(2,1)S(1)} %collective-permute-done.5.refs_4_), channel_id=1, source_target_pairs={{0,16},{16,0},{32,48},{48,32},{64,80},{80,64},{96,112},{112,96},{1... | collective-permute-start | bytes 393224 | tf_op jit(solution)/shard_map/ppermute | solution.py:23
  41.8 2.5 %collective-permute-start.16 = (bf16[256,128]{1,0:T(8,128)(2,1)S(1)}, bf16[256,128]{1,0:T(8,128)(2,1)S(1)}, u32[]{:S(2)}, u32[]{:S(2)}) collective-permute-start(bf16[256,128]{1,0:T(8,128)(2,1)S(1)} %fusion.refs_0_), channel_id=1, source_target_pairs={{0,128},{16,144},{32,160},{48,176},{64,192},{80,208},{96,224},{112... | collective-permute-start | bytes 196616 | tf_op jit(solution)/shard_map/ppermute | solution.py:23
  44.3 4.0 %forward_transform.1 = (f32[2,256,256]{2,1,0:T(8,128)S(1)}, f32[4,256,128]{2,1,0:T(8,128)S(1)}, f32[4,256,128]{2,1,0:T(8,128)S(1)}) custom-call(f32[128]{0:T(128)S(1)} %dynamic-slice_bitcast_fusion.1.turn_ref, f32[8,128]{1,0:T(8,128)S(1)} %dynamic-slice_bitcast_fusion.twid_ref, bf16[2,256,256]{2,1,0:T(8,128)(2,1)S(1)} %copy-done.4, ...), custom_call_target="tpu_custom_call" | custom-call | flops 2000000000 | bytes 4194304 | tf_op jit(solution)/shard_map/forward_transform/pallas_call | solution.py:174
  48.9 2.3 %collective-permute-start.17 = (f32[4,256,128]{2,1,0:T(8,128)S(1)}, f32[4,256,128]{2,1,0:T(8,128)S(1)}, u32[]{:S(2)}, u32[]{:S(2)}) collective-permute-start(f32[4,256,128]{2,1,0:T(8,128)S(1)} %get-tuple-element.89), channel_id=1, source_target_pairs={{0,16},{16,0},{32,48},{48,32},{64,80},{80,64},{96,112},{112,96},{1... | collective-permute-start | bytes 1572872 | tf_op jit(solution)/shard_map/ppermute | solution.py:23
  51.7 3.5 %collective-permute-start.25 = (bf16[2,256,128]{2,1,0:T(8,128)(2,1)S(1)}, bf16[2,256,128]{2,1,0:T(8,128)(2,1)S(1)}, u32[]{:S(2)}, u32[]{:S(2)}) collective-permute-start(bf16[2,256,128]{2,1,0:T(8,128)(2,1)S(1)} %pad_maximum_fusion.2), channel_id=1, source_target_pairs={{0,64},{16,80},{32,96},{48,112},{64,0},{80,16},{96,32},{112,48},{1... | collective-permute-start | bytes 393224 | tf_op jit(solution)/shard_map/ppermute | solution.py:23
  55.3 2.8 %collective-permute-start.20 = (bf16[256,128]{1,0:T(8,128)(2,1)S(1)}, bf16[256,128]{1,0:T(8,128)(2,1)S(1)}, u32[]{:S(2)}, u32[]{:S(2)}) collective-permute-start(bf16[256,128]{1,0:T(8,128)(2,1)S(1)} %get-tuple-element.93), channel_id=1, source_target_pairs={{0,96},{16,112},{32,64},{48,80},{64,32},{80,48},{96,0},{112,16},{1... | collective-permute-start | bytes 196616 | tf_op jit(solution)/shard_map/ppermute | solution.py:23
  58.8 3.0 %collective-permute-done.25.refs_3_ = bf16[2,256,128]{2,1,0:T(8,128)(2,1)S(1)} collective-permute-done((bf16[2,256,128]{2,1,0:T(8,128)(2,1)S(1)}, bf16[2,256,128]{2,1,0:T(8,128)(2,1)S(1)}, u32[]{:S(2)}, u32[]{:S(2)}) %collective-permute-start.25) | collective-permute-done | bytes 131104 | tf_op jit(solution)/shard_map/ppermute | solution.py:23
  62.6 3.1 %collective-permute-done.26.refs_4_ = bf16[2,256,128]{2,1,0:T(8,128)(2,1)S(1)} collective-permute-done((bf16[2,256,128]{2,1,0:T(8,128)(2,1)S(1)}, bf16[2,256,128]{2,1,0:T(8,128)(2,1)S(1)}, u32[]{:S(2)}, u32[]{:S(2)}) %collective-permute-start.26) | collective-permute-done | bytes 131104 | tf_op jit(solution)/shard_map/ppermute | solution.py:23
  72.8 4.1 %backward_transform.1 = (f32[2,2,256,128]{3,2,1,0:T(8,128)S(1)}, f32[4,256,128]{2,1,0:T(8,128)S(1)}, f32[4,256,128]{2,1,0:T(8,128)S(1)}) custom-call(f32[128]{0:T(128)S(1)} %dynamic-slice_bitcast_fusion.1.turn_ref, f32[8,128]{1,0:T(8,128)S(1)} %dynamic-slice_bitcast_fusion.twid_ref, bf16[2,256,256]{2,1,0:T(8,128)(2,1)S(1)} %copy-done.4, ...), custom_call_target="tpu_custom_call" | custom-call | flops 2000000000 | bytes 4194304 | tf_op jit(solution)/shard_map/backward_transform/pallas_call | solution.py:174
  81.0 2.7 %collective-permute-start.36 = (bf16[256,128]{1,0:T(8,128)(2,1)S(1)}, bf16[256,128]{1,0:T(8,128)(2,1)S(1)}, u32[]{:S(2)}, u32[]{:S(2)}) collective-permute-start(bf16[256,128]{1,0:T(8,128)(2,1)S(1)} %get-tuple-element.102), channel_id=1, source_target_pairs={{0,32},{16,48},{32,0},{48,16},{64,96},{80,112},{96,64},{112,80},{1... | collective-permute-start | bytes 196616 | tf_op jit(solution)/shard_map/ppermute | solution.py:23
  84.1 2.1 %collective-permute-start.33 = (bf16[4,256,128]{2,1,0:T(8,128)(2,1)S(1)}, bf16[4,256,128]{2,1,0:T(8,128)(2,1)S(1)}, u32[]{:S(2)}, u32[]{:S(2)}) collective-permute-start(bf16[4,256,128]{2,1,0:T(8,128)(2,1)S(1)} %pad_maximum_fusion.refs_0_), channel_id=1, source_target_pairs={{0,2},{1,3},{2,0},{3,1},{4,6},{5,7},{6,4},{7,5},{8,10},{9,11},{10,... | collective-permute-start | bytes 786440 | tf_op jit(solution)/shard_map/ppermute | solution.py:23
  88.3 2.0 %collective-permute-done.32.refs_1_ = bf16[4,256,128]{2,1,0:T(8,128)(2,1)S(1)} collective-permute-done((bf16[4,256,128]{2,1,0:T(8,128)(2,1)S(1)}, bf16[4,256,128]{2,1,0:T(8,128)(2,1)S(1)}, u32[]{:S(2)}, u32[]{:S(2)}) %collective-permute-start.32) | collective-permute-done | bytes 262176 | tf_op jit(solution)/shard_map/ppermute | solution.py:23
  90.3 6.7 %collective-permute-done.33.refs_2_ = bf16[4,256,128]{2,1,0:T(8,128)(2,1)S(1)} collective-permute-done((bf16[4,256,128]{2,1,0:T(8,128)(2,1)S(1)}, bf16[4,256,128]{2,1,0:T(8,128)(2,1)S(1)}, u32[]{:S(2)}, u32[]{:S(2)}) %collective-permute-start.33) | collective-permute-done | bytes 262176 | tf_op jit(solution)/shard_map/ppermute | solution.py:23
  97.0 2.7 %collective-permute-done.34.refs_3_ = bf16[4,256,128]{2,1,0:T(8,128)(2,1)S(1)} collective-permute-done((bf16[4,256,128]{2,1,0:T(8,128)(2,1)S(1)}, bf16[4,256,128]{2,1,0:T(8,128)(2,1)S(1)}, u32[]{:S(2)}, u32[]{:S(2)}) %collective-permute-start.34) | collective-permute-done | bytes 262176 | tf_op jit(solution)/shard_map/ppermute | solution.py:23
  100.9 1.7 %project_output.1 = bf16[128,256]{1,0:T(8,128)(2,1)} custom-call(s32[2]{0:T(128)S(1)} %pad_add_fusion.place_ref, bf16[4096,256]{1,0:T(8,128)(2,1)S(1)} %copy-done.1, bf16[4,256,128]{2,1,0:T(8,128)(2,1)S(1)} %pad_maximum_fusion.refs_0_, bf16[4,256,128]{2,1,0:T(8,128)(2,1)S(1)} %collective-permute-done.32.refs_1_, ...), custom_call_target="tpu_custom_call" | custom-call | flops 268000000 | bytes 3145728 | tf_op jit(solution)/shard_map/project_output/pallas_call | solution.py:271
  (90 shorter events, 28.6 us)
Async XLA Ops:
  4.4 12.6 %collective-permute-start = (bf16[4,256,128]{2,1,0:T(8,128)(2,1)S(1)}, bf16[4,256,128]{2,1,0:T(8,128)(2,1)S(1)}, u32[]{:S(2)}, u32[]{:S(2)}) collective-permute-start(bf16[4,256,128]{2,1,0:T(8,128)(2,1)S(1)} %get-tuple-element.58), channel_id=1, source_target_pairs={{0,1},{1,0},{2,3},{3,2},{4,5},{5,4},{6,7},{7,6},{8,9},{9,8},{10,11... | collective-permute-start | bytes 786440 | tf_op jit(solution)/shard_map/ppermute | solution.py:23
  6.6 10.5 %collective-permute-start.1 = (bf16[4,256,128]{2,1,0:T(8,128)(2,1)S(1)}, bf16[4,256,128]{2,1,0:T(8,128)(2,1)S(1)}, u32[]{:S(2)}, u32[]{:S(2)}) collective-permute-start(bf16[4,256,128]{2,1,0:T(8,128)(2,1)S(1)} %get-tuple-element.59), channel_id=1, source_target_pairs={{0,3},{1,2},{2,1},{3,0},{4,7},{5,6},{6,5},{7,4},{8,11},{9,10},{10,... | collective-permute-start | bytes 786440 | tf_op jit(solution)/shard_map/ppermute | solution.py:23
  8.4 8.6 %collective-permute-start.2 = (bf16[256,128]{1,0:T(8,128)(2,1)S(1)}, bf16[256,128]{1,0:T(8,128)(2,1)S(1)}, u32[]{:S(2)}, u32[]{:S(2)}) collective-permute-start(bf16[256,128]{1,0:T(8,128)(2,1)S(1)} %copy-done.2), channel_id=1, source_target_pairs={{0,128},{16,144},{32,160},{48,176},{64,192},{80,208},{96,224},{112... | collective-permute-start | bytes 196616 | tf_op jit(solution)/shard_map/ppermute | solution.py:23
  15.3 7.8 %collective-permute-start.12 = (bf16[4,256,128]{2,1,0:T(8,128)(2,1)S(1)}, bf16[4,256,128]{2,1,0:T(8,128)(2,1)S(1)}, u32[]{:S(2)}, u32[]{:S(2)}) collective-permute-start(bf16[4,256,128]{2,1,0:T(8,128)(2,1)S(1)} %get-tuple-element.69), channel_id=1, source_target_pairs={{0,2},{1,3},{2,0},{3,1},{4,6},{5,7},{6,4},{7,5},{8,10},{9,11},{10,... | collective-permute-start | bytes 786440 | tf_op jit(solution)/shard_map/ppermute | solution.py:23
  16.0 12.4 %collective-permute-start.6 = (bf16[2,2,256,128]{3,2,1,0:T(8,128)(2,1)S(1)}, bf16[2,2,256,128]{3,2,1,0:T(8,128)(2,1)S(1)}, u32[]{:S(2)}, u32[]{:S(2)}) collective-permute-start(bf16[2,2,256,128]{3,2,1,0:T(8,128)(2,1)S(1)} %bitcast.28), channel_id=1, source_target_pairs={{0,128},{16,144},{32,160},{48,176},{64,192},{80,208},{96,224},{112... | collective-permute-start | bytes 786440 | tf_op jit(solution)/shard_map/ppermute | solution.py:23
  17.0 17.1 %collective-permute-start.3 = (bf16[2,256,128]{2,1,0:T(8,128)(2,1)S(1)}, bf16[2,256,128]{2,1,0:T(8,128)(2,1)S(1)}, u32[]{:S(2)}, u32[]{:S(2)}) collective-permute-start(bf16[2,256,128]{2,1,0:T(8,128)(2,1)S(1)} %pad_maximum_fusion.1), channel_id=1, source_target_pairs={{0,32},{16,48},{32,0},{48,16},{64,96},{80,112},{96,64},{112,80},{1... | collective-permute-start | bytes 393224 | tf_op jit(solution)/shard_map/ppermute | solution.py:23
  18.4 16.4 %collective-permute-start.4 = (bf16[2,256,128]{2,1,0:T(8,128)(2,1)S(1)}, bf16[2,256,128]{2,1,0:T(8,128)(2,1)S(1)}, u32[]{:S(2)}, u32[]{:S(2)}) collective-permute-start(bf16[2,256,128]{2,1,0:T(8,128)(2,1)S(1)} %pad_maximum_fusion.1), channel_id=1, source_target_pairs={{0,64},{16,80},{32,96},{48,112},{64,0},{80,16},{96,32},{112,48},{1... | collective-permute-start | bytes 393224 | tf_op jit(solution)/shard_map/ppermute | solution.py:23
  21.0 13.8 %collective-permute-start.5 = (bf16[2,256,128]{2,1,0:T(8,128)(2,1)S(1)}, bf16[2,256,128]{2,1,0:T(8,128)(2,1)S(1)}, u32[]{:S(2)}, u32[]{:S(2)}) collective-permute-start(bf16[2,256,128]{2,1,0:T(8,128)(2,1)S(1)} %pad_maximum_fusion.1), channel_id=1, source_target_pairs={{0,96},{16,112},{32,64},{48,80},{64,32},{80,48},{96,0},{112,16},{1... | collective-permute-start | bytes 393224 | tf_op jit(solution)/shard_map/ppermute | solution.py:23
  23.2 14.2 %collective-permute-start.15 = (bf16[256,128]{1,0:T(8,128)(2,1)S(1)}, bf16[256,128]{1,0:T(8,128)(2,1)S(1)}, u32[]{:S(2)}, u32[]{:S(2)}) collective-permute-start(bf16[256,128]{1,0:T(8,128)(2,1)S(1)} %get-tuple-element.74), channel_id=1, source_target_pairs={{0,12},{1,13},{2,14},{3,15},{4,8},{5,9},{6,10},{7,11},{8,4},{9,5},... | collective-permute-start | bytes 196616 | tf_op jit(solution)/shard_map/ppermute | solution.py:23
  28.4 9.4 %collective-permute-start.14 = (bf16[256,128]{1,0:T(8,128)(2,1)S(1)}, bf16[256,128]{1,0:T(8,128)(2,1)S(1)}, u32[]{:S(2)}, u32[]{:S(2)}) collective-permute-start(bf16[256,128]{1,0:T(8,128)(2,1)S(1)} %get-tuple-element.73), channel_id=1, source_target_pairs={{0,8},{1,9},{2,10},{3,11},{4,12},{5,13},{6,14},{7,15},{8,0},{9,1},... | collective-permute-start | bytes 196616 | tf_op jit(solution)/shard_map/ppermute | solution.py:23
  41.8 7.1 %collective-permute-start.16 = (bf16[256,128]{1,0:T(8,128)(2,1)S(1)}, bf16[256,128]{1,0:T(8,128)(2,1)S(1)}, u32[]{:S(2)}, u32[]{:S(2)}) collective-permute-start(bf16[256,128]{1,0:T(8,128)(2,1)S(1)} %fusion.refs_0_), channel_id=1, source_target_pairs={{0,128},{16,144},{32,160},{48,176},{64,192},{80,208},{96,224},{112... | collective-permute-start | bytes 196616 | tf_op jit(solution)/shard_map/ppermute | solution.py:23
  51.2 6.8 %collective-permute-start.24 = (bf16[2,256,128]{2,1,0:T(8,128)(2,1)S(1)}, bf16[2,256,128]{2,1,0:T(8,128)(2,1)S(1)}, u32[]{:S(2)}, u32[]{:S(2)}) collective-permute-start(bf16[2,256,128]{2,1,0:T(8,128)(2,1)S(1)} %pad_maximum_fusion.2), channel_id=1, source_target_pairs={{0,32},{16,48},{32,0},{48,16},{64,96},{80,112},{96,64},{112,80},{1... | collective-permute-start | bytes 393224 | tf_op jit(solution)/shard_map/ppermute | solution.py:23
  51.7 10.1 %collective-permute-start.25 = (bf16[2,256,128]{2,1,0:T(8,128)(2,1)S(1)}, bf16[2,256,128]{2,1,0:T(8,128)(2,1)S(1)}, u32[]{:S(2)}, u32[]{:S(2)}) collective-permute-start(bf16[2,256,128]{2,1,0:T(8,128)(2,1)S(1)} %pad_maximum_fusion.2), channel_id=1, source_target_pairs={{0,64},{16,80},{32,96},{48,112},{64,0},{80,16},{96,32},{112,48},{1... | collective-permute-start | bytes 393224 | tf_op jit(solution)/shard_map/ppermute | solution.py:23
  55.2 10.5 %collective-permute-start.26 = (bf16[2,256,128]{2,1,0:T(8,128)(2,1)S(1)}, bf16[2,256,128]{2,1,0:T(8,128)(2,1)S(1)}, u32[]{:S(2)}, u32[]{:S(2)}) collective-permute-start(bf16[2,256,128]{2,1,0:T(8,128)(2,1)S(1)} %pad_maximum_fusion.2), channel_id=1, source_target_pairs={{0,96},{16,112},{32,64},{48,80},{64,32},{80,48},{96,0},{112,16},{1... | collective-permute-start | bytes 393224 | tf_op jit(solution)/shard_map/ppermute | solution.py:23
  55.3 11.8 %collective-permute-start.20 = (bf16[256,128]{1,0:T(8,128)(2,1)S(1)}, bf16[256,128]{1,0:T(8,128)(2,1)S(1)}, u32[]{:S(2)}, u32[]{:S(2)}) collective-permute-start(bf16[256,128]{1,0:T(8,128)(2,1)S(1)} %get-tuple-element.93), channel_id=1, source_target_pairs={{0,96},{16,112},{32,64},{48,80},{64,32},{80,48},{96,0},{112,16},{1... | collective-permute-start | bytes 196616 | tf_op jit(solution)/shard_map/ppermute | solution.py:23
  58.1 9.8 %collective-permute-start.19 = (bf16[256,128]{1,0:T(8,128)(2,1)S(1)}, bf16[256,128]{1,0:T(8,128)(2,1)S(1)}, u32[]{:S(2)}, u32[]{:S(2)}) collective-permute-start(bf16[256,128]{1,0:T(8,128)(2,1)S(1)} %get-tuple-element.92), channel_id=1, source_target_pairs={{0,64},{16,80},{32,96},{48,112},{64,0},{80,16},{96,32},{112,48},{1... | collective-permute-start | bytes 196616 | tf_op jit(solution)/shard_map/ppermute | solution.py:23
  58.1 9.8 %collective-permute-start.18 = (bf16[256,128]{1,0:T(8,128)(2,1)S(1)}, bf16[256,128]{1,0:T(8,128)(2,1)S(1)}, u32[]{:S(2)}, u32[]{:S(2)}) collective-permute-start(bf16[256,128]{1,0:T(8,128)(2,1)S(1)} %get-tuple-element.91), channel_id=1, source_target_pairs={{0,32},{16,48},{32,0},{48,16},{64,96},{80,112},{96,64},{112,80},{1... | collective-permute-start | bytes 196616 | tf_op jit(solution)/shard_map/ppermute | solution.py:23
  61.7 7.4 %collective-permute-start.27 = (bf16[256,128]{1,0:T(8,128)(2,1)S(1)}, bf16[256,128]{1,0:T(8,128)(2,1)S(1)}, u32[]{:S(2)}, u32[]{:S(2)}) collective-permute-start(bf16[256,128]{1,0:T(8,128)(2,1)S(1)} %fusion.refs_0_), channel_id=1, source_target_pairs={{0,16},{16,0},{32,48},{48,32},{64,80},{80,64},{96,112},{112,96},{1... | collective-permute-start | bytes 196616 | tf_op jit(solution)/shard_map/ppermute | solution.py:23
  69.1 7.8 %collective-permute-start.23 = (bf16[256,128]{1,0:T(8,128)(2,1)S(1)}, bf16[256,128]{1,0:T(8,128)(2,1)S(1)}, u32[]{:S(2)}, u32[]{:S(2)}) collective-permute-start(bf16[256,128]{1,0:T(8,128)(2,1)S(1)} %fusion.1), channel_id=1, source_target_pairs={{0,12},{1,13},{2,14},{3,15},{4,8},{5,9},{6,10},{7,11},{8,4},{9,5},... | collective-permute-start | bytes 196616 | tf_op jit(solution)/shard_map/ppermute | solution.py:23
  70.0 7.8 %collective-permute-start.22 = (bf16[256,128]{1,0:T(8,128)(2,1)S(1)}, bf16[256,128]{1,0:T(8,128)(2,1)S(1)}, u32[]{:S(2)}, u32[]{:S(2)}) collective-permute-start(bf16[256,128]{1,0:T(8,128)(2,1)S(1)} %fusion.1), channel_id=1, source_target_pairs={{0,8},{1,9},{2,10},{3,11},{4,12},{5,13},{6,14},{7,15},{8,0},{9,1},... | collective-permute-start | bytes 196616 | tf_op jit(solution)/shard_map/ppermute | solution.py:23
  80.5 7.1 %collective-permute-start.37 = (bf16[256,128]{1,0:T(8,128)(2,1)S(1)}, bf16[256,128]{1,0:T(8,128)(2,1)S(1)}, u32[]{:S(2)}, u32[]{:S(2)}) collective-permute-start(bf16[256,128]{1,0:T(8,128)(2,1)S(1)} %get-tuple-element.103), channel_id=1, source_target_pairs={{0,64},{16,80},{32,96},{48,112},{64,0},{80,16},{96,32},{112,48},{1... | collective-permute-start | bytes 196616 | tf_op jit(solution)/shard_map/ppermute | solution.py:23
  83.7 6.6 %collective-permute-start.32 = (bf16[4,256,128]{2,1,0:T(8,128)(2,1)S(1)}, bf16[4,256,128]{2,1,0:T(8,128)(2,1)S(1)}, u32[]{:S(2)}, u32[]{:S(2)}) collective-permute-start(bf16[4,256,128]{2,1,0:T(8,128)(2,1)S(1)} %pad_maximum_fusion.refs_0_), channel_id=1, source_target_pairs={{0,1},{1,0},{2,3},{3,2},{4,5},{5,4},{6,7},{7,6},{8,9},{9,8},{10,11... | collective-permute-start | bytes 786440 | tf_op jit(solution)/shard_map/ppermute | solution.py:23
  84.1 12.9 %collective-permute-start.33 = (bf16[4,256,128]{2,1,0:T(8,128)(2,1)S(1)}, bf16[4,256,128]{2,1,0:T(8,128)(2,1)S(1)}, u32[]{:S(2)}, u32[]{:S(2)}) collective-permute-start(bf16[4,256,128]{2,1,0:T(8,128)(2,1)S(1)} %pad_maximum_fusion.refs_0_), channel_id=1, source_target_pairs={{0,2},{1,3},{2,0},{3,1},{4,6},{5,7},{6,4},{7,5},{8,10},{9,11},{10,... | collective-permute-start | bytes 786440 | tf_op jit(solution)/shard_map/ppermute | solution.py:23
  86.2 13.4 %collective-permute-start.34 = (bf16[4,256,128]{2,1,0:T(8,128)(2,1)S(1)}, bf16[4,256,128]{2,1,0:T(8,128)(2,1)S(1)}, u32[]{:S(2)}, u32[]{:S(2)}) collective-permute-start(bf16[4,256,128]{2,1,0:T(8,128)(2,1)S(1)} %pad_maximum_fusion.refs_0_), channel_id=1, source_target_pairs={{0,3},{1,2},{2,1},{3,0},{4,7},{5,6},{6,5},{7,4},{8,11},{9,10},{10,... | collective-permute-start | bytes 786440 | tf_op jit(solution)/shard_map/ppermute | solution.py:23
  (23 other events, 214.7 us)
